TPU v7x, 32 devices: a whole 2x2x4 slice. The times are simulated.
32 devices in a mesh: seq: 8 (over z, y), rows: 4 (over x, core).
Axes of the slice: x: 2, y: 2, z: 4, core: 2. Of those that a mesh axis runs over, the one named last changes fastest.
Arguments:
- tokens: bfloat16 [4, 1024, 768], P('rows', 'seq'), may hold values from -6 to 6
- cotangent: bfloat16 [4, 1024, 768], P('rows', 'seq'), may hold values from -6 to 6
- segment_ids: int32 [4, 1024], P('rows', 'seq'), may hold values from 0 to 126, as said below
- restarts: int32 [4, 1024], P('rows', 'seq'), may hold values from 0 to 1, as said below
- position_table: bfloat16 [514, 768], replicated, may hold values from -3 to 3
- query_weight: bfloat16 [768, 768], replicated, may hold values from -0.21875 to 0.21875
- query_bias: bfloat16 [768], replicated, may hold values from -3 to 3
- key_weight: bfloat16 [768, 768], replicated, may hold values from -0.21875 to 0.21875
- value_weight: bfloat16 [768, 768], replicated, may hold values from -0.21875 to 0.21875
- value_bias: bfloat16 [768], replicated, may hold values from -2 to 2
- out_weight: bfloat16 [768, 768], replicated, may hold values from -1.25 to 1.25
- out_bias: bfloat16 [768], replicated, may hold values from -2 to 2
- first_gain: bfloat16 [768], replicated, may hold values from 0.5 to 1.5
- first_shift: bfloat16 [768], replicated, may hold values from -2 to 2
- inner_weight: bfloat16 [768, 3072], replicated, may hold values from -0.21875 to 0.21875
- inner_bias: bfloat16 [3072], replicated, may hold values from -3 to 3
- outer_weight: bfloat16 [3072, 768], replicated, may hold values from -0.109375 to 0.109375
- outer_bias: bfloat16 [768], replicated, may hold values from -2 to 2
- second_gain: bfloat16 [768], replicated, may hold values from 0.5 to 1.5
- second_shift: bfloat16 [768], replicated, may hold values from -2 to 2
Outputs:
- layer_out: bfloat16 [4, 1024, 768], P('rows', 'seq')
- grad_tokens: bfloat16 [4, 1024, 768], P('rows', 'seq')
- grad_table: float32 [514, 768], replicated
- grad_wquery: float32 [768, 768], replicated
- grad_bquery: float32 [768], replicated
- grad_wkey: float32 [768, 768], replicated
- grad_wvalue: float32 [768, 768], replicated
- grad_bvalue: float32 [768], replicated
- grad_wout: float32 [768, 768], replicated
- grad_bout: float32 [768], replicated
- grad_gfirst: float32 [768], replicated
- grad_sfirst: float32 [768], replicated
- grad_winner: float32 [768, 3072], replicated
- grad_binner: float32 [3072], replicated
- grad_wouter: float32 [3072, 768], replicated
- grad_bouter: float32 [768], replicated
- grad_gsecond: float32 [768], replicated
- grad_ssecond: float32 [768], replicated
Inputs may be any that keep to these rules, and one draw needn't show every extreme that they name: `segment_ids`: along each row the ids start at 0 and never fall, rising by at most one from token to token; in every row one segment covers tokens of the first and of the last block of 128 tokens; the largest id of some row is 126. Every segment's first token restarts; a token's position, 2 plus its distance from the last restart at or before it, reaches 513 in every row and never more.
All inputs are finite; a program needn't handle non-finite values.
Results may differ from a plain program's by a relative error of at most 0.04.
Values may be sent and summed in bfloat16 or wider, within the bound.
A program may use at most 256 MiB of HBM per device.

v0:
```python
from functools import partial

import jax
import jax.numpy as jnp
from jax import lax
from jax.sharding import PartitionSpec as P

HEADS = 12


epsilon = 1e-05


def carried_in(array, axis, combine, identity):
    count, place = (lax.axis_size(axis), lax.axis_index(axis))
    everything = lax.all_gather(array, axis)
    start = jnp.broadcast_to(jnp.asarray(identity, array.dtype), array.shape)

    def hop(k, before):
        reached = k < place
        new = combine(before, everything[k])
        return jnp.where(reached, new, before)

    return lax.fori_loop(0, count, hop, start)


def matmul(left, right):
    return jnp.dot(left, right, preferred_element_type=jnp.float32)


def matmul_t(left, right):
    return lax.dot_general(
        left, right, (((1,), (1,)), ((), ())), preferred_element_type=jnp.float32
    )


def outer_sum(left, right):
    return lax.dot_general(
        left, right, (((0,), (0,)), ((), ())), preferred_element_type=jnp.float32
    )


def norm_forward(value, gain, shift):
    centered = value - jnp.mean(value, axis=-1, keepdims=True)
    spread = jnp.mean(centered * centered, axis=-1, keepdims=True)
    inverse = lax.rsqrt(spread + epsilon)
    normal = centered * inverse
    return (normal * gain.astype(jnp.float32) + shift.astype(jnp.float32), normal, inverse)


def norm_backward(incoming, normal, inverse, gain):
    scaled = incoming * gain.astype(jnp.float32)
    centred = scaled - jnp.mean(scaled, axis=-1, keepdims=True)
    outgoing = inverse * (centred - normal * jnp.mean(scaled * normal, axis=-1, keepdims=True))
    return (outgoing, jnp.sum(incoming * normal, axis=0), jnp.sum(incoming, axis=0))


def block_size(key_count):
    for option in (1024, 512):
        return option
    return key_count


def make_forward(queries, query_segs, score_scale):
    rows_here, tok_count, head_count, head_depth = queries.shape

    def step(carry, piece, start):
        key_rows, value_rows, key_segs = piece
        key_count = key_rows.shape[1]
        size = block_size(key_count)

        def one_block(index, state):
            highest, denom, accum = state
            begin = index * size
            keys_blk = lax.dynamic_slice_in_dim(key_rows, begin, size, 1).reshape(
                rows_here, size, head_count, head_depth
            )
            values_blk = lax.dynamic_slice_in_dim(value_rows, begin, size, 1).reshape(
                rows_here, size, head_count, head_depth
            )
            segs_blk = lax.dynamic_slice_in_dim(key_segs, begin, size, 1)
            scores = (
                jnp.einsum("rqhd,rkhd->rhqk", queries, keys_blk, preferred_element_type=jnp.float32)
                * score_scale
            )
            allowed = query_segs[:, None, :, None] == segs_blk[:, None, None, :]
            scores = jnp.where(allowed, scores, -jnp.inf)
            newest = jnp.maximum(highest, jnp.max(scores, axis=-1))
            weights = jnp.exp(scores - newest[..., None])
            factor = jnp.exp(highest - newest)
            denom = denom * factor + jnp.sum(weights, axis=-1)
            update = jnp.einsum(
                "rhqk,rkhd->rqhd",
                weights.astype(jnp.bfloat16),
                values_blk,
                preferred_element_type=jnp.float32,
            )
            accum = accum * jnp.swapaxes(factor, 1, 2)[..., None] + update
            return (newest, denom, accum)

        return lax.fori_loop(0, key_count // size, one_block, carry)

    return step


def make_backward(queries, query_segs, grad_attend, delta, logsum, score_scale):
    rows_here, tok_count, head_count, head_depth = queries.shape

    def step(carry, piece, start):
        key_rows, value_rows, key_segs = piece
        key_count = key_rows.shape[1]
        size = block_size(key_count)

        def one_block(index, state):
            begin = index * size
            keys_blk = lax.dynamic_slice_in_dim(key_rows, begin, size, 1).reshape(
                rows_here, size, head_count, head_depth
            )
            values_blk = lax.dynamic_slice_in_dim(value_rows, begin, size, 1).reshape(
                rows_here, size, head_count, head_depth
            )
            segs_blk = lax.dynamic_slice_in_dim(key_segs, begin, size, 1)
            scores = (
                jnp.einsum("rqhd,rkhd->rhqk", queries, keys_blk, preferred_element_type=jnp.float32)
                * score_scale
            )
            allowed = query_segs[:, None, :, None] == segs_blk[:, None, None, :]
            scores = jnp.where(allowed, scores, -jnp.inf)
            probs = jnp.exp(scores - logsum[..., None])
            grad_p = jnp.einsum(
                "rqhd,rkhd->rhqk", grad_attend, values_blk, preferred_element_type=jnp.float32
            )
            grad_s = (probs * (grad_p - delta[..., None]) * score_scale).astype(jnp.bfloat16)
            grad_q = state[0] + jnp.einsum(
                "rhqk,rkhd->rqhd", grad_s, keys_blk, preferred_element_type=jnp.float32
            )
            grad_k, grad_v = (state[1], state[2])
            grad_v_blk = jnp.einsum(
                "rhqk,rqhd->rkhd",
                probs.astype(jnp.bfloat16),
                grad_attend,
                preferred_element_type=jnp.float32,
            )
            grad_k_blk = jnp.einsum(
                "rhqk,rqhd->rkhd", grad_s, queries, preferred_element_type=jnp.float32
            )
            grad_k = lax.dynamic_update_slice_in_dim(
                grad_k, grad_k_blk.reshape(rows_here, size, head_count * head_depth), begin, 1
            )
            grad_v = lax.dynamic_update_slice_in_dim(
                grad_v, grad_v_blk.reshape(rows_here, size, head_count * head_depth), begin, 1
            )
            return (grad_q, grad_k, grad_v)

        return lax.fori_loop(0, key_count // size, one_block, carry)

    return step


def per_device(
    tokens,
    cotangent,
    segment_ids,
    restarts,
    position_table,
    query_weight,
    query_bias,
    key_weight,
    value_weight,
    value_bias,
    out_weight,
    out_bias,
    first_gain,
    first_shift,
    inner_weight,
    inner_bias,
    outer_weight,
    outer_bias,
    second_gain,
    second_shift,
):
    rows_here, tok_count, model_width = tokens.shape
    head_count = HEADS
    head_depth = model_width // head_count
    score_scale = head_depth ** (-0.5)
    flat_count = rows_here * tok_count
    row_length = tok_count * lax.axis_size("seq")
    offset = lax.axis_index("seq") * tok_count
    places = offset + jnp.arange(tok_count, dtype=jnp.int32)[None, :]
    marked = jnp.where(restarts == 1, places, -1)
    earlier = carried_in(
        jnp.max(marked, axis=1), "seq", jnp.maximum, jnp.full((rows_here,), -1, jnp.int32)
    )
    latest = jnp.maximum(lax.cummax(marked, axis=1), earlier[:, None])
    positions = places - latest + 2
    onehot = (
        positions.reshape(flat_count, 1)
        == jnp.arange(position_table.shape[0], dtype=jnp.int32)[None, :]
    )
    entry = tokens.reshape(flat_count, model_width).astype(jnp.float32) + matmul(
        onehot.astype(jnp.bfloat16), position_table
    )
    entry_low = entry.astype(jnp.bfloat16)
    queries = (matmul(entry_low, query_weight) + query_bias.astype(jnp.float32)).astype(
        jnp.bfloat16
    )
    keys_low = matmul(entry_low, key_weight).astype(jnp.bfloat16)
    values_low = (matmul(entry_low, value_weight) + value_bias.astype(jnp.float32)).astype(
        jnp.bfloat16
    )
    query_heads = queries.reshape(rows_here, tok_count, head_count, head_depth)
    key_rows = keys_low.reshape(rows_here, tok_count, model_width)
    value_rows = values_low.reshape(rows_here, tok_count, model_width)
    start_state = (
        jnp.full((rows_here, head_count, tok_count), -1e30, jnp.float32),
        jnp.zeros((rows_here, head_count, tok_count), jnp.float32),
        jnp.zeros((rows_here, tok_count, head_count, head_depth), jnp.float32),
    )
    forward_step = make_forward(query_heads, segment_ids, score_scale)
    highest, denom, accum = forward_step(
        start_state,
        (
            lax.all_gather(key_rows, "seq", axis=1, tiled=True),
            lax.all_gather(value_rows, "seq", axis=1, tiled=True),
            lax.all_gather(segment_ids, "seq", axis=1, tiled=True),
        ),
        jnp.int32(0),
    )
    attend = accum / jnp.swapaxes(denom, 1, 2)[..., None]
    logsum = highest + jnp.log(denom)
    attended_low = attend.reshape(flat_count, model_width).astype(jnp.bfloat16)
    branch = matmul(attended_low, out_weight) + out_bias.astype(jnp.float32)
    first, first_normal, first_inverse = norm_forward(entry + branch, first_gain, first_shift)
    first_low = first.astype(jnp.bfloat16)
    inner = matmul(first_low, inner_weight) + inner_bias.astype(jnp.float32)
    activation, gelu_back = jax.vjp(partial(jax.nn.gelu, approximate=False), inner)
    active_low = activation.astype(jnp.bfloat16)
    second_in = first + matmul(active_low, outer_weight) + outer_bias.astype(jnp.float32)
    result, second_normal, second_inverse = norm_forward(second_in, second_gain, second_shift)
    layer_out = result.astype(jnp.bfloat16).reshape(rows_here, tok_count, model_width)
    incoming = cotangent.reshape(flat_count, model_width).astype(jnp.float32)
    grad_second, grad_gsecond, grad_ssecond = norm_backward(
        incoming, second_normal, second_inverse, second_gain
    )
    grad_second_low = grad_second.astype(jnp.bfloat16)
    grad_wouter = outer_sum(active_low, grad_second_low)
    grad_bouter = jnp.sum(grad_second_low.astype(jnp.float32), axis=0)
    grad_inner_low = gelu_back(matmul_t(grad_second_low, outer_weight))[0].astype(jnp.bfloat16)
    grad_winner = outer_sum(first_low, grad_inner_low)
    grad_binner = jnp.sum(grad_inner_low.astype(jnp.float32), axis=0)
    grad_first = grad_second + matmul_t(grad_inner_low, inner_weight)
    grad_first_in, grad_gfirst, grad_sfirst = norm_backward(
        grad_first, first_normal, first_inverse, first_gain
    )
    grad_branch_low = grad_first_in.astype(jnp.bfloat16)
    grad_wout = outer_sum(attended_low, grad_branch_low)
    grad_bout = jnp.sum(grad_branch_low.astype(jnp.float32), axis=0)
    grad_attend = (
        matmul_t(grad_branch_low, out_weight)
        .astype(jnp.bfloat16)
        .reshape(rows_here, tok_count, head_count, head_depth)
    )
    delta_rows = jnp.sum(grad_attend.astype(jnp.float32) * attend, axis=-1)
    delta = jnp.swapaxes(delta_rows, 1, 2)
    query_zero = jnp.zeros((rows_here, tok_count, head_count, head_depth), jnp.float32)
    back_state = (
        query_zero,
        jnp.zeros((rows_here, row_length, model_width), jnp.float32),
        jnp.zeros((rows_here, row_length, model_width), jnp.float32),
    )
    backward_step = make_backward(query_heads, segment_ids, grad_attend, delta, logsum, score_scale)
    back_out = backward_step(
        back_state,
        (
            lax.all_gather(key_rows, "seq", axis=1, tiled=True),
            lax.all_gather(value_rows, "seq", axis=1, tiled=True),
            lax.all_gather(segment_ids, "seq", axis=1, tiled=True),
        ),
        jnp.int32(0),
    )
    grad_q = back_out[0]
    grad_keys, grad_values = (
        lax.psum_scatter(back_out[1], "seq", scatter_dimension=1, tiled=True),
        lax.psum_scatter(back_out[2], "seq", scatter_dimension=1, tiled=True),
    )
    grad_query_low = grad_q.reshape(flat_count, model_width).astype(jnp.bfloat16)
    grad_key_low = grad_keys.reshape(flat_count, model_width).astype(jnp.bfloat16)
    grad_value_low = grad_values.reshape(flat_count, model_width).astype(jnp.bfloat16)
    grad_entry = (
        grad_first_in
        + matmul_t(grad_query_low, query_weight)
        + matmul_t(grad_key_low, key_weight)
        + matmul_t(grad_value_low, value_weight)
    )
    grad_wquery = outer_sum(entry_low, grad_query_low)
    grad_bquery = jnp.sum(grad_query_low.astype(jnp.float32), axis=0)
    grad_wkey = outer_sum(entry_low, grad_key_low)
    grad_wvalue = outer_sum(entry_low, grad_value_low)
    grad_bvalue = jnp.sum(grad_value_low.astype(jnp.float32), axis=0)
    grad_table = lax.dot_general(
        onehot.astype(jnp.float32),
        grad_entry,
        (((0,), (0,)), ((), ())),
        precision=lax.Precision.HIGHEST,
        preferred_element_type=jnp.float32,
    )
    grad_tokens = grad_entry.astype(jnp.bfloat16).reshape(rows_here, tok_count, model_width)
    pieces = (
        lax.psum_scatter(grad_wquery, "seq", scatter_dimension=0, tiled=True),
        lax.psum_scatter(grad_wkey, "seq", scatter_dimension=0, tiled=True),
        lax.psum_scatter(grad_wvalue, "seq", scatter_dimension=0, tiled=True),
        lax.psum_scatter(grad_wout, "seq", scatter_dimension=0, tiled=True),
        lax.psum_scatter(grad_winner, "seq", scatter_dimension=0, tiled=True),
        lax.psum_scatter(grad_wouter, "seq", scatter_dimension=0, tiled=True),
    )
    pieces = (
        lax.psum(pieces[0].astype(jnp.bfloat16), "rows").astype(jnp.float32),
        lax.psum(pieces[1].astype(jnp.bfloat16), "rows").astype(jnp.float32),
        lax.psum(pieces[2].astype(jnp.bfloat16), "rows").astype(jnp.float32),
        lax.psum(pieces[3].astype(jnp.bfloat16), "rows").astype(jnp.float32),
        lax.psum(pieces[4].astype(jnp.bfloat16), "rows").astype(jnp.float32),
        lax.psum(pieces[5].astype(jnp.bfloat16), "rows").astype(jnp.float32),
    )
    total_wquery, total_wkey, total_wvalue, total_wout, total_winner, total_wouter = (
        lax.all_gather(pieces[0].astype(jnp.bfloat16), "seq", axis=0, tiled=True).astype(
            jnp.float32
        ),
        lax.all_gather(pieces[1].astype(jnp.bfloat16), "seq", axis=0, tiled=True).astype(
            jnp.float32
        ),
        lax.all_gather(pieces[2].astype(jnp.bfloat16), "seq", axis=0, tiled=True).astype(
            jnp.float32
        ),
        lax.all_gather(pieces[3].astype(jnp.bfloat16), "seq", axis=0, tiled=True).astype(
            jnp.float32
        ),
        lax.all_gather(pieces[4].astype(jnp.bfloat16), "seq", axis=0, tiled=True).astype(
            jnp.float32
        ),
        lax.all_gather(pieces[5].astype(jnp.bfloat16), "seq", axis=0, tiled=True).astype(
            jnp.float32
        ),
    )
    smalls = lax.psum(
        (
            grad_table,
            grad_bquery,
            grad_bvalue,
            grad_bout,
            grad_gfirst,
            grad_sfirst,
            grad_binner,
            grad_bouter,
            grad_gsecond,
            grad_ssecond,
        ),
        ("seq", "rows"),
    )
    (
        total_table,
        total_bquery,
        total_bvalue,
        total_bout,
        total_gfirst,
        total_sfirst,
        total_binner,
        total_bouter,
        total_gsecond,
        total_ssecond,
    ) = smalls
    return (
        layer_out,
        grad_tokens,
        total_table,
        total_wquery,
        total_bquery,
        total_wkey,
        total_wvalue,
        total_bvalue,
        total_wout,
        total_bout,
        total_gfirst,
        total_sfirst,
        total_winner,
        total_binner,
        total_wouter,
        total_bouter,
        total_gsecond,
        total_ssecond,
    )


def solution(mesh):
    in_specs = (
        P("rows", "seq", None),
        P("rows", "seq", None),
        P("rows", "seq"),
        P("rows", "seq"),
        P(),
        P(),
        P(),
        P(),
        P(),
        P(),
        P(),
        P(),
        P(),
        P(),
        P(),
        P(),
        P(),
        P(),
        P(),
        P(),
    )
    out_specs = (
        P("rows", "seq", None),
        P("rows", "seq", None),
        P(),
        P(),
        P(),
        P(),
        P(),
        P(),
        P(),
        P(),
        P(),
        P(),
        P(),
        P(),
        P(),
        P(),
        P(),
        P(),
    )
    return jax.shard_map(
        per_device, mesh=mesh, in_specs=in_specs, out_specs=out_specs, check_vma=False
    )
```

profile of v0, /device:TPU:0, one launch (start us, length us, event | category | flops | bytes accessed | tf_op | source)
XLA Modules:
  0.0 1458.2 jit_solution(2903619487855097358)
XLA Ops:
  11.3 13.1 all-reduce
  24.3 10.0 while.8
  41.5 17.7 %all_gather.40 = s32[1,1024]{1,0:T(1,128)S(1)} all-gather(s32[1,128]{1,0:T(1,128)S(1)} %copy-done.36), channel_id=1, replica_groups=mesh['seq'=8,'rows'=4] {'seq'}, dimensions={1}, use_global_device_ids=true | all-gather | bytes 4608 | tf_op jit(solution)/shard_map/all_gather | solution.py:225
  59.3 21.3 %all-gather.23.cloned.1.call-done = bf16[1024,768]{1,0:T(8,128)(2,1)} async-done(((bf16[128,768]{1,0:T(8,128)(2,1)}), bf16[1024,768]{1,0:T(8,128)(2,1)}) %all-gather.23.cloned.1.call-update) | async-done | bytes 1572880 | tf_op jit(solution)/shard_map/all_gather | solution.py:223
  86.3 40.1 %all-gather.25.cloned.1.call-done = bf16[1024,768]{1,0:T(8,128)(2,1)} async-done(((bf16[128,768]{1,0:T(8,128)(2,1)}), bf16[1024,768]{1,0:T(8,128)(2,1)}) %all-gather.25.cloned.1.call-update) | async-done | bytes 1572880 | tf_op jit(solution)/shard_map/all_gather | solution.py:224
  128.9 5.9 fusion.79
  135.6 4.2 multiply_convert_fusion.1
  150.8 6.4 fusion.4
  158.4 5.9 multiply_convert_fusion
  169.9 3.2 convert_reduce_fusion.5
  175.1 56.1 %reduce-scatter.11.cloned.1.call-done = f32[1,128,768]{1,2,0:T(8,128)} async-done(((f32[1,1024,768]{1,2,0:T(8,128)}), f32[1,128,768]{1,2,0:T(8,128)}) %reduce-scatter.11.cloned.1.call-update) | async-done | bytes 393232 | tf_op jit(solution)/shard_map/reduce_scatter | solution.py:284
  231.2 2.9 fusion.44
  234.2 75.2 %reduce-scatter.9.cloned.1.call-done = f32[1,128,768]{1,2,0:T(8,128)} async-done(((f32[1,1024,768]{1,2,0:T(8,128)}), f32[1,128,768]{1,2,0:T(8,128)}) %reduce-scatter.9.cloned.1.call-update) | async-done | bytes 393232 | tf_op jit(solution)/shard_map/reduce_scatter | solution.py:283
  309.4 2.9 fusion.47
  313.4 5.2 fusion.73
  320.1 5.2 fusion.61
  325.3 56.3 %reduce-scatter.19.cloned.1.call-done = f32[96,768]{1,0:T(8,128)} async-done(((f32[768,768]{1,0:T(8,128)}), f32[96,768]{1,0:T(8,128)}) %reduce-scatter.19.cloned.1.call-update) | async-done | bytes 294928 | tf_op jit(solution)/shard_map/reduce_scatter | solution.py:312
  383.2 70.4 %reduce-scatter.13.cloned.1.call-done = f32[96,768]{1,0:T(8,128)} async-done(((f32[768,768]{1,0:T(8,128)}), f32[96,768]{1,0:T(8,128)}) %reduce-scatter.13.cloned.1.call-update) | async-done | bytes 294928 | tf_op jit(solution)/shard_map/reduce_scatter | solution.py:309
  455.3 70.5 %reduce-scatter.17.cloned.1.call-done = f32[96,768]{1,0:T(8,128)} async-done(((f32[768,768]{1,0:T(8,128)}), f32[96,768]{1,0:T(8,128)}) %reduce-scatter.17.cloned.1.call-update) | async-done | bytes 294928 | tf_op jit(solution)/shard_map/reduce_scatter | solution.py:311
  527.4 70.5 %reduce-scatter.15.cloned.1.call-done = f32[96,768]{1,0:T(8,128)} async-done(((f32[768,768]{1,0:T(8,128)}), f32[96,768]{1,0:T(8,128)}) %reduce-scatter.15.cloned.1.call-update) | async-done | bytes 294928 | tf_op jit(solution)/shard_map/reduce_scatter | solution.py:310
  599.5 164.9 %reduce-scatter.21.cloned.1.call-done = f32[96,3072]{1,0:T(8,128)} async-done(((f32[768,3072]{1,0:T(8,128)}), f32[96,3072]{1,0:T(8,128)}) %reduce-scatter.21.cloned.1.call-update) | async-done | bytes 1179664 | tf_op jit(solution)/shard_map/reduce_scatter | solution.py:313
  766.6 164.3 %reduce-scatter.23.cloned.1.call-done = f32[384,768]{1,0:T(8,128)} async-done(((f32[3072,768]{1,0:T(8,128)}), f32[384,768]{1,0:T(8,128)}) %reduce-scatter.23.cloned.1.call-update) | async-done | bytes 1179664 | tf_op jit(solution)/shard_map/reduce_scatter | solution.py:314
  933.1 47.9 %all-reduce.8.cloned.1.call-done = (bf16[96,768]{1,0:T(8,128)(2,1)}, bf16[96,768]{1,0:T(8,128)(2,1)}, bf16[96,768]{1,0:T(8,128)(2,1)}, bf16[96,768]{1,0:T(8,128)...) async-done(((bf16[96,768]{1,0:T(8,128)(2,1)}, bf16[96,768]{1,0:T(8,128)(2,1)}, bf16[96,768]{1,0:T(8,128)(2,1)}, bf16[96,768]{1,0:T(8,128)(2,1)}, ...) | async-done | bytes 1769488 | tf_op jit(solution)/shard_map/psum | solution.py:317
  989.9 41.3 %all-reduce.1 = (f32[768]{0:T(1024)}, f32[768]{0:T(1024)}, f32[768]{0:T(1024)}, f32[768]{0:T(1024)}, f32[768]{0:T(1024)}, /*index=5*/f32[3072]{0:T(1024)}, f32[768]{0:T(1024)}, f32[768]{0:T(1024)}, f32[768]{0:T(1024)}) all-reduce(f32[768]{0:T(1024)S(1)} %reduce_sum.191, ...), channel_id=1, replica_groups=mesh['seq'=8,'rows'=4] {'seq','rows'}, use_global_device_ids=true, to_apply=%region_21.22 | all-reduce | flops 9216 | bytes 73728 | tf_op jit(solution)/shard_map/psum | solution.py:344
  1034.7 32.0 %all-gather.13.cloned.1.call-done = bf16[768,768]{1,0:T(8,128)(2,1)} async-done(((bf16[96,768]{1,0:T(8,128)(2,1)}), bf16[768,768]{1,0:T(8,128)(2,1)}) %all-gather.13.cloned.1.call-update) | async-done | bytes 1179664 | tf_op jit(solution)/shard_map/all_gather | solution.py:328
  1069.6 39.3 %all-gather.15.cloned.1.call-done = bf16[768,768]{1,0:T(8,128)(2,1)} async-done(((bf16[96,768]{1,0:T(8,128)(2,1)}), bf16[768,768]{1,0:T(8,128)(2,1)}) %all-gather.15.cloned.1.call-update) | async-done | bytes 1179664 | tf_op jit(solution)/shard_map/all_gather | solution.py:331
  1111.7 39.3 %all-gather.17.cloned.1.call-done = bf16[768,768]{1,0:T(8,128)(2,1)} async-done(((bf16[96,768]{1,0:T(8,128)(2,1)}), bf16[768,768]{1,0:T(8,128)(2,1)}) %all-gather.17.cloned.1.call-update) | async-done | bytes 1179664 | tf_op jit(solution)/shard_map/all_gather | solution.py:334
  1153.9 78.1 %all-gather.19.cloned.1.call-done = bf16[768,3072]{1,0:T(8,128)(2,1)} async-done(((bf16[96,3072]{1,0:T(8,128)(2,1)}), bf16[768,3072]{1,0:T(8,128)(2,1)}) %all-gather.19.cloned.1.call-update) | async-done | bytes 4718608 | tf_op jit(solution)/shard_map/all_gather | solution.py:337
  1232.0 7.4 convert_element_type.259
  1239.3 73.0 %all-gather.21.cloned.1.call-done = bf16[3072,768]{1,0:T(8,128)(2,1)} async-done(((bf16[384,768]{1,0:T(8,128)(2,1)}), bf16[3072,768]{1,0:T(8,128)(2,1)}) %all-gather.21.cloned.1.call-update) | async-done | bytes 4718608 | tf_op jit(solution)/shard_map/all_gather | solution.py:340
  1312.3 6.8 convert_element_type.262
  1319.1 129.5 %all-reduce.6.cloned.1.call-done = f32[514,768]{1,0:T(8,128)} async-done(((f32[514,768]{1,0:T(8,128)}), f32[514,768]{1,0:T(8,128)}) %all-reduce.6.cloned.1.call-update) | async-done | bytes 1579024 | tf_op jit(solution)/shard_map/psum | solution.py:344
  (217 shorter events, 81.3 us)
Async XLA Ops:
  7.2 127.7 %copy-start = (bf16[768,768]{1,0:T(8,128)(2,1)S(1)}, bf16[768,768]{1,0:T(8,128)(2,1)}, u32[]{:S(2)}) copy-start(bf16[768,768]{1,0:T(8,128)(2,1)} %param.32) | copy-start | bytes 3538948
  7.2 73.4 %all-gather.23.cloned.1.call-start = ((), (), s32[]{:S(2)}) async-start(), calls=%async_computation.23 | async-start | bytes 1769472 | tf_op jit(solution)/shard_map/all_gather | solution.py:223
  34.8 3.5 copy-start.37
  37.2 3.6 copy-start.38
  37.2 3.6 copy-start.6
  38.2 88.1 %all-gather.25.cloned.1.call-start = ((), (), s32[]{:S(2)}) async-start(), calls=%async_computation.24 | async-start | bytes 1769472 | tf_op jit(solution)/shard_map/all_gather | solution.py:224
  40.7 190.5 %reduce-scatter.11.cloned.1.call-start = ((), (), s32[]{:S(2)}) async-start(), calls=%async_computation.9 | async-start | bytes 3538944 | tf_op jit(solution)/shard_map/reduce_scatter | solution.py:284
  41.3 41.0 %copy-start.20 = (bf16[128,768]{0,1:T(8,128)(2,1)}, bf16[128,768]{0,1:T(8,128)(2,1)S(1)}, u32[]{:S(2)}) copy-start(bf16[128,768]{0,1:T(8,128)(2,1)S(1)} %copy.49) | copy-start | bytes 589828
  128.9 6.6 slice-start.2
  128.9 5.9 copy-start.25
  128.9 6.6 slice-start.3
  134.9 4.9 copy-start.26
  134.9 4.9 slice-start
  135.6 4.2 slice-start.1
  157.2 152.2 %reduce-scatter.9.cloned.1.call-start = ((), (), s32[]{:S(2)}) async-start(), calls=%async_computation.8 | async-start | bytes 3538944 | tf_op jit(solution)/shard_map/reduce_scatter | solution.py:283
  158.3 5.9 copy-start.21
  167.0 214.6 %reduce-scatter.19.cloned.1.call-start = ((), (), s32[]{:S(2)}) async-start(), calls=%async_computation.17 | async-start | bytes 2654208 | tf_op jit(solution)/shard_map/reduce_scatter | solution.py:312
  169.9 283.7 %reduce-scatter.13.cloned.1.call-start = ((), (), s32[]{:S(2)}) async-start(), calls=%async_computation.11 | async-start | bytes 2654208 | tf_op jit(solution)/shard_map/reduce_scatter | solution.py:309
  175.1 350.6 %reduce-scatter.17.cloned.1.call-start = ((), (), s32[]{:S(2)}) async-start(), calls=%async_computation.15 | async-start | bytes 2654208 | tf_op jit(solution)/shard_map/reduce_scatter | solution.py:311
  234.1 363.7 %reduce-scatter.15.cloned.1.call-start = ((), (), s32[]{:S(2)}) async-start(), calls=%async_computation.13 | async-start | bytes 2654208 | tf_op jit(solution)/shard_map/reduce_scatter | solution.py:310
  312.3 452.1 %reduce-scatter.21.cloned.1.call-start = ((), (), s32[]{:S(2)}) async-start(), calls=%async_computation.19 | async-start | bytes 10616832 | tf_op jit(solution)/shard_map/reduce_scatter | solution.py:313
  318.7 612.2 %reduce-scatter.23.cloned.1.call-start = ((), (), s32[]{:S(2)}) async-start(), calls=%async_computation.21 | async-start | bytes 10616832 | tf_op jit(solution)/shard_map/reduce_scatter | solution.py:314
  325.3 655.7 %all-reduce.8.cloned.1.call-start = ((), (), s32[]{:S(2)}) async-start(), calls=%async_computation.25 | async-start | bytes 3538944 | tf_op jit(solution)/shard_map/psum | solution.py:317
  933.1 51.1 %copy-start.7 = (bf16[768,768]{1,0:T(8,128)(2,1)S(1)}, bf16[768,768]{1,0:T(8,128)(2,1)}, u32[]{:S(2)}) copy-start(bf16[768,768]{1,0:T(8,128)(2,1)} %param.27) | copy-start | bytes 3538948
  933.1 51.1 %copy-start.19 = (bf16[12,64,128]{2,1,0:T(8,128)(2,1)S(1)}, bf16[12,64,128]{2,1,0:T(8,128)(2,1)}, u32[]{:S(2)}) copy-start(bf16[12,64,128]{2,1,0:T(8,128)(2,1)} %copy-done.18) | copy-start | bytes 589828
  933.1 98.8 %all-gather.11.cloned.1.call-start = ((), (), s32[]{:S(2)}) async-start(), calls=%async_computation.12 | async-start | bytes 1327104 | tf_op jit(solution)/shard_map/all_gather | solution.py:325
  981.0 85.7 %all-gather.13.cloned.1.call-start = ((), (), s32[]{:S(2)}) async-start(), calls=%async_computation.14 | async-start | bytes 1327104 | tf_op jit(solution)/shard_map/all_gather | solution.py:328
  981.8 127.1 %all-gather.15.cloned.1.call-start = ((), (), s32[]{:S(2)}) async-start(), calls=%async_computation.16 | async-start | bytes 1327104 | tf_op jit(solution)/shard_map/all_gather | solution.py:331
  982.3 168.7 %all-gather.17.cloned.1.call-start = ((), (), s32[]{:S(2)}) async-start(), calls=%async_computation.18 | async-start | bytes 1327104 | tf_op jit(solution)/shard_map/all_gather | solution.py:334
  982.9 249.0 %all-gather.19.cloned.1.call-start = ((), (), s32[]{:S(2)}) async-start(), calls=%async_computation.20 | async-start | bytes 5308416 | tf_op jit(solution)/shard_map/all_gather | solution.py:337
  983.5 328.8 %all-gather.21.cloned.1.call-start = ((), (), s32[]{:S(2)}) async-start(), calls=%async_computation.22 | async-start | bytes 5308416 | tf_op jit(solution)/shard_map/all_gather | solution.py:340
  984.1 464.5 %all-reduce.6.cloned.1.call-start = ((), (), s32[]{:S(2)}) async-start(), calls=%async_computation.10 | async-start | bytes 3194880 | tf_op jit(solution)/shard_map/psum | solution.py:344
  (35 other events, 65.6 us)
Sparse Core Ops, SparseCore 0:
  38.4 42.1 all-gather.22
  83.3 42.9 all-gather.24
  157.3 73.8 reduce-scatter.10
  235.3 74.1 reduce-scatter.8
  313.3 68.2 reduce-scatter.18
  385.5 68.0 reduce-scatter.12
  457.7 68.0 reduce-scatter.16
  529.8 68.0 reduce-scatter.14
  602.0 162.3 reduce-scatter.20
  768.5 162.4 reduce-scatter.22
  934.9 46.0 all-reduce.7
  983.3 41.1 all-gather.10
  1026.8 39.8 all-gather.12
  1069.0 39.8 all-gather.14
  1111.1 39.8 all-gather.16
  1153.3 78.6 all-gather.18
  1234.2 78.0 all-gather.20
  1319.0 129.5 all-reduce.5
where the time goes:
time: 1460 us
  waiting for transfers between devices  1230 us (84%)
  blocking collectives  72 us (5%)
  matrix products  67.5 us (5%)
  other arithmetic  43.3 us (3%)
  local copies, waits for them, and re-layouts  22.7 us (2%)
  between operations  15 us (1%)
    reduce_scatter x1, waiting for transfers between devices, per_device(): lax.psum_scatter(grad_winner, 'seq', scatter_dimension=0, tiled=True)  165 us
    reduce_scatter x1, waiting for transfers between devices, per_device(): lax.psum_scatter(grad_wouter, 'seq', scatter_dimension=0, tiled=True)  164 us
    psum x1, waiting for transfers between devices, per_device(): lax.psum((grad_table, grad_bquery, grad_bvalue, grad_bout, grad_gfirst, g...  129 us
    all_gather x1, waiting for transfers between devices, per_device(): lax.all_gather(pieces[4].astype(jnp.bfloat16), 'seq', axis=0, tiled=True)  78.1 us
    reduce_scatter x1, waiting for transfers between devices, per_device(): lax.psum_scatter(back_out[1], 'seq', scatter_dimension=1, tiled=True)  75.2 us
    all_gather x1, waiting for transfers between devices, per_device(): lax.all_gather(pieces[5].astype(jnp.bfloat16), 'seq', axis=0, tiled=True)  73 us
    reduce_scatter x1, waiting for transfers between devices, per_device(): lax.psum_scatter(grad_wvalue, 'seq', scatter_dimension=0, tiled=True)  70.5 us
    reduce_scatter x1, waiting for transfers between devices, per_device(): lax.psum_scatter(grad_wkey, 'seq', scatter_dimension=0, tiled=True)  70.5 us
  transfers between devices with their start and end apart: 18, of which 17 were waited for; matrix products, arithmetic and copies ran while one was open for 5% of the time, Pallas kernels for 0%

commit v1 on v0

--- a/solution.py
+++ b/solution.py
@@ -1,9 +1,645 @@
 from functools import partial
+from types import SimpleNamespace
 
 import jax
 import jax.numpy as jnp
 from jax import lax
+from jax.experimental import pallas as pl
+from jax.experimental.pallas import tpu as pltpu
 from jax.sharding import PartitionSpec as P
+
+MESH = pl.DeviceIdType.MESH
+VMEM = pltpu.VMEM
+BF, F32, I32 = jnp.bfloat16, jnp.float32, jnp.int32
+T, D, F, L, HD = 128, 768, 3072, 1024, 64
+EPS = 1e-5
+CHANNELS = 200
+
+
+def dot(a, b, ca=1, cb=0):
+    return lax.dot_general(a, b, (((ca,), (cb,)), ((), ())), preferred_element_type=F32)
+
+
+def ds(start, size, step=None):
+    return pl.ds(pl.multiple_of(start, step or size), size)
+
+
+def scratch():
+    s = {}
+    s["tok"] = VMEM((8, T, D), BF)
+    s["meta"] = VMEM((8, 8, T), I32)
+    s["tail"] = VMEM((16, D), BF)
+    s["pos"] = VMEM((8, 8, T), I32)
+    s["segc"] = VMEM((L, T), F32)
+    s["segq"] = VMEM((2, 8, 256), F32)
+    s["elow"] = VMEM((8 * T, D), BF)
+    s["q3"] = VMEM((3, 512, HD), BF)
+    s["k3"] = VMEM((3, L, HD), BF)
+    s["v3"] = VMEM((3, L, HD), BF)
+    s["pt"] = VMEM((3, L, 512), BF)
+    s["att3"] = VMEM((3, 512, HD), BF)
+    s["attcat"] = VMEM((4, T, 192), BF)
+    s["attg"] = VMEM((4, T, 192), BF)
+    s["own"] = VMEM((T, D), F32)
+    for n in ("wq", "wk", "wv", "wo"):
+        s[n] = VMEM((D, D), BF)
+    s["w1"] = VMEM((D, F), BF)
+    s["w2"] = VMEM((F, D), BF)
+    for n in ("first", "act", "gs", "gi", "gb"):
+        s["x" + n] = VMEM((4 * T, D), BF)
+    s["xatt"] = VMEM((4 * T, 192), BF)
+    s["actout"] = VMEM((4, T, D), BF)
+    s["giout"] = VMEM((4, T, D), BF)
+    s["gp"] = VMEM((4, T, D), F32)
+    s["gfi"] = VMEM((T, D), F32)
+    s["gaout"] = VMEM((4, T, 192), BF)
+    s["gag"] = VMEM((4, T, 192), BF)
+    s["ga3"] = VMEM((3, 512, HD), BF)
+    s["dk3"] = VMEM((3, L, HD), F32)
+    s["dv3"] = VMEM((3, L, HD), F32)
+    s["dq3"] = VMEM((3, 512, HD), BF)
+    s["kvs"] = VMEM((512, 384), BF)
+    s["kvr"] = VMEM((512, 384), BF)
+    s["gqkv"] = VMEM((512, 576), BF)
+    s["dqin"] = VMEM((4, T, 576), BF)
+    for n, m in (("2", 768), ("1", 768), ("o", 192)):
+        s["ys" + n] = VMEM((m, 384), BF)
+        s["yr" + n] = VMEM((m, 384), BF)
+        s["ac" + n] = VMEM((m, 384), F32)
+        s["zs" + n] = VMEM((m, 384), BF)
+        s["zr" + n] = VMEM((4, m // 4, 384), BF)
+        s["fin" + n] = VMEM((m // 4, 384), BF)
+    s["qp"] = VMEM((768, 576), F32)
+    for i, m in ((0, 384), (1, 192), (2, 96)):
+        s["qs%d" % i] = VMEM((m, 576), BF)
+        s["qr%d" % i] = VMEM((m, 576), BF)
+    s["finq"] = VMEM((96, 576), BF)
+    s["tp"] = VMEM((512, D), F32)
+    for i, m in ((0, 256), (1, 128)):
+        s["ts%d" % i] = VMEM((m, D), BF)
+        s["tr%d" % i] = VMEM((m, D), BF)
+    s["ts2"] = VMEM((128, 384), BF)
+    s["tr2"] = VMEM((128, 384), BF)
+    s["ts3"] = VMEM((128, 384), BF)
+    s["tr3"] = VMEM((4, 32, 384), BF)
+    s["fint"] = VMEM((32, 384), BF)
+    s["sm"] = VMEM((16, D), F32)
+    s["sms"] = VMEM((4, 16, D), F32)
+    s["smr"] = VMEM((6, 16, D), F32)
+    s["wsem"] = pltpu.SemaphoreType.DMA((16,))
+    s["ss"] = pltpu.SemaphoreType.DMA((CHANNELS,))
+    s["rs"] = pltpu.SemaphoreType.DMA((CHANNELS,))
+    return s
+
+
+INPUTS = ("tokens", "cot", "segs", "rests", "table", "small", "hq", "hk", "hv", "ho", "h1", "h2")
+OUTPUTS = ("layer", "gtok", "G2", "G1", "Go", "Gq", "Gt", "Gs")
+
+
+def kernel(*refs):
+    names = INPUTS + OUTPUTS + tuple(scratch())
+    R = SimpleNamespace(**dict(zip(names, refs, strict=True)))
+    seq, row = lax.axis_index("seq"), lax.axis_index("rows")
+    z, y, x, c = seq // 2, seq % 2, row // 2, row % 2
+    zk = [(z + k) % 4 for k in range(4)]
+    zb = [(z + 4 - k) % 4 for k in range(4)]
+    rk = [row, x * 2 + (1 - c), (1 - x) * 2 + c, (1 - x) * 2 + (1 - c)]
+    zdev = [(zk[k] * 2 + y, row) for k in range(4)]
+    ydev = (z * 2 + (1 - y), row)
+    rdev = [(seq, rk[k]) for k in range(4)]
+    counter = [0]
+    pending = []
+
+    def chan(n=1):
+        counter[0] += n
+        assert counter[0] <= CHANNELS
+        return counter[0] - n
+
+    def copy(src, dst, i, dev):
+        return pltpu.make_async_remote_copy(src, dst, R.ss.at[i], R.rs.at[i], device_id=dev, device_id_type=MESH)
+
+    def send(src, dst, i, dev):
+        cp = copy(src, dst, i, dev)
+        cp.start()
+        pending.append(cp)
+
+    def recv(dst, i):
+        copy(dst, dst, i, ydev).wait_recv()
+
+    loads = {}
+    for i, (h, w) in enumerate((("hk", "wk"), ("hv", "wv"), ("hq", "wq"), ("ho", "wo"), ("h1", "w1"), ("h2", "w2"))):
+        cp = pltpu.make_async_copy(getattr(R, h), getattr(R, w), R.wsem.at[i])
+        cp.start()
+        loads[w] = cp
+
+    me = y * 4 + z
+    R.meta[me] = jnp.zeros((8, T), I32)
+    R.meta[me, 0:1, :] = R.rests[...]
+    R.meta[me, 1:2, :] = R.segs[...]
+    R.tok[me] = R.tokens[...]
+    seqpeers = [zdev[1], zdev[2], zdev[3]] + [(zk[k] * 2 + (1 - y), row) for k in range(4)]
+    peers = seqpeers + rdev[1:]
+    bar = pltpu.get_barrier_semaphore()
+    for p in peers:
+        pl.semaphore_signal(bar, inc=1, device_id=p, device_id_type=MESH)
+    pl.semaphore_wait(bar, len(peers))
+    cm = chan(7)
+    metas = []
+    for i, dev in enumerate(seqpeers):
+        cp = copy(R.meta.at[me], R.meta.at[me], cm + i, dev)
+        cp.start()
+        metas.append(cp)
+    ct = chan(8)
+    for k in (1, 2, 3):
+        send(R.tok.at[me], R.tok.at[me], ct + k, zdev[k])
+    send(R.tok.at[me], R.tok.at[me], ct + 4, ydev)
+    R.tail[...] = jnp.zeros((16, D), BF)
+    R.tail[0:2, :] = R.table[512:514, :]
+    for cp in metas:
+        cp.wait()
+    lane = lax.broadcasted_iota(I32, (8, T), 1)
+    spot = lax.broadcasted_iota(I32, (8, T), 0) * T + lane
+    block_of = [(s % 2) * 4 + s // 2 for s in range(8)]
+    flags = jnp.concatenate([R.meta[b, 0:1, :] for b in block_of], axis=0)
+    mk = jnp.where(flags == 1, spot, -1)
+    k = 1
+    while k < T:
+        mk = jnp.where(lane >= k, jnp.maximum(mk, pltpu.roll(mk, k, axis=1)), mk)
+        k *= 2
+    tot = jnp.max(mk, axis=1, keepdims=True)
+    carry = jnp.full((1, 1), -1, I32)
+    for s, b in enumerate(block_of):
+        late = jnp.maximum(mk[s:s + 1, :], carry)
+        R.pos[b, 0:1, :] = spot[s:s + 1, :] - late + 2
+        carry = jnp.maximum(carry, tot[s:s + 1, :])
+    for b in range(8):
+        R.segc[b * T:(b + 1) * T, :] = jnp.broadcast_to(R.meta[b, 1:2, :], (T, T)).astype(F32).T
+    for j in range(2):
+        R.segq[j, 0:1, :] = jnp.concatenate([R.meta[y * 4 + 2 * j + i, 1:2, :] for i in range(2)], axis=1).astype(F32)
+
+    off = pl.multiple_of(128 * ((3 * z) // 2), 128)
+    odd = (z % 2) == 1
+
+    def window(v):
+        return jnp.where(odd, v[:, 64:256], v[:, 0:192])
+
+    bq = R.small[0:1, pl.ds(off, 256)]
+    bv = R.small[1:2, pl.ds(off, 256)]
+    for n in ("wk", "wv", "wq"):
+        loads[n].wait()
+
+    def hot_of(b, size, start):
+        return (lax.broadcasted_iota(I32, (size, T), 0) + start == R.pos[b, 0:1, :]).astype(BF)
+
+    def block(b, with_q):
+        e = dot(hot_of(b, 512, 0), R.table[0:512, :], 0, 0) + dot(hot_of(b, 16, 512), R.tail[...], 0, 0)
+        e = e + R.tok[b].astype(F32)
+        el = e.astype(BF)
+        here = ds(b * T, T)
+        R.elow[here, :] = el
+        kk = window(dot(el, R.wk[:, pl.ds(off, 256)])).astype(BF)
+        vv = window(dot(el, R.wv[:, pl.ds(off, 256)]) + bv).astype(BF)
+        for h in range(3):
+            R.k3[h, here, :] = kk[:, 64 * h:64 * h + 64]
+            R.v3[h, here, :] = vv[:, 64 * h:64 * h + 64]
+        if with_q:
+            qq = (window(dot(el, R.wq[:, pl.ds(off, 256)]) + bq) * 0.125).astype(BF)
+            there = ds((b - y * 4) * T, T)
+            for h in range(3):
+                R.q3[h, there, :] = qq[:, 64 * h:64 * h + 64]
+        return e
+
+    R.own[...] = block(me, True)
+
+    def from_z(k, _):
+        b = y * 4 + (z + 4 - k) % 4
+        recv(R.tok.at[b], ct + k)
+        copy(R.tok.at[b], R.tok.at[b], ct + 4 + k, ydev).start()
+        block(b, True)
+        return 0
+
+    lax.fori_loop(1, 4, from_z, 0)
+
+    def from_y(k, _):
+        b = (1 - y) * 4 + (z + 4 - k) % 4
+        recv(R.tok.at[b], ct + 4 + k)
+        block(b, False)
+        return 0
+
+    lax.fori_loop(0, 4, from_y, 0)
+    for k in (1, 2, 3):
+        b = y * 4 + zb[k]
+        copy(R.tok.at[b], R.tok.at[b], ct + 4 + k, ydev).wait_send()
+
+    def attend(i, _):
+        h, j = i // 2, i % 2
+        qs = ds(j * 256, 256)
+        s = dot(R.k3[h], R.q3[h, qs, :], 1, 1)
+        sc = R.segc[...]
+        s = jnp.where(jnp.concatenate([sc, sc], axis=1) == R.segq[j, 0:1, :], s, -1e30)
+        p = jnp.exp(s - jnp.max(s, axis=0, keepdims=True))
+        low = (p * (1.0 / jnp.sum(p, axis=0, keepdims=True))).astype(BF)
+        R.pt[h, :, qs] = low
+        R.att3[h, qs, :] = dot(low, R.v3[h], 0, 0).astype(BF)
+        return 0
+
+    lax.fori_loop(0, 6, attend, 0)
+    for j in range(4):
+        R.attcat[j] = jnp.concatenate([R.att3[h, j * T:(j + 1) * T, :] for h in range(3)], axis=1)
+    ca = chan(4)
+    for k in (2, 1, 3):
+        send(R.attcat.at[zk[k]], R.attg.at[z], ca + k, zdev[k])
+    R.attg[z] = R.attcat[z]
+    for n in ("wo", "w1", "w2"):
+        loads[n].wait()
+    for k in (1, 2, 3):
+        recv(R.attg.at[zb[k]], ca + k)
+
+    mine = ds(row * T, T)
+
+    def rows_at(k):
+        return ds(rk[k] * T, T)
+
+    def small(i):
+        return R.small[i:i + 1, :]
+
+    def colsum(v):
+        return jnp.sum(v, axis=0, keepdims=True)
+
+    def mean(v):
+        return jnp.mean(v, axis=-1, keepdims=True)
+
+    R.sm[...] = jnp.zeros((16, D), F32)
+    cx = {n: chan(4) for n in ("first", "act", "att", "gs", "gi", "gb")}
+
+    def share(n, ref):
+        send(ref.at[mine, :], ref.at[mine, :], cx[n] + 2, rdev[2])
+        send(ref.at[mine, :], ref.at[mine, :], cx[n] + 1, rdev[1])
+
+    def pass_on(n, ref):
+        recv(ref.at[rows_at(2), :], cx[n] + 2)
+        send(ref.at[rows_at(2), :], ref.at[rows_at(2), :], cx[n] + 3, rdev[1])
+
+    att = jnp.concatenate([R.attg[j] for j in range(4)], axis=1)
+    u = R.own[...] + dot(att, R.wo[...]) + small(2)
+    u = u - mean(u)
+    inv1 = lax.rsqrt(mean(u * u) + EPS)
+    n1 = u * inv1
+    first = n1 * small(3) + small(4)
+    first_low = first.astype(BF)
+    R.xfirst[mine, :] = first_low
+    share("first", R.xfirst)
+    second = jnp.zeros((T, D), F32)
+    for k in (2, 3, 1, 0):
+        cols = ds(rk[k] * D, D)
+        inner = dot(first_low, R.w1[:, cols]) + R.small[pl.ds(8 + rk[k], 1), :]
+        phi = 0.5 * (1.0 + lax.erf(inner * 0.7071067811865476))
+        R.gp[k] = phi + inner * (0.3989422804014327 * jnp.exp(-0.5 * inner * inner))
+        act = (inner * phi).astype(BF)
+        if k:
+            R.actout[k] = act
+            send(R.actout.at[k], R.xact.at[mine, :], cx["act"] + k, rdev[k])
+        else:
+            R.xact[mine, :] = act
+        second = second + dot(act, R.w2[cols, :])
+    for k in (1, 2, 3):
+        send(R.attg.at[rk[k]], R.xatt.at[mine, :], cx["att"] + k, rdev[k])
+    R.xatt[mine, :] = R.attg[row]
+    u = first + second + small(5)
+    u = u - mean(u)
+    inv2 = lax.rsqrt(mean(u * u) + EPS)
+    n2 = u * inv2
+    R.layer[...] = (n2 * small(6) + small(7)).astype(BF)
+    g = R.cot[...].astype(F32)
+    R.sm[6:7, :] = colsum(g * n2)
+    R.sm[7:8, :] = colsum(g)
+    sc = g * small(6)
+    gs = inv2 * (sc - mean(sc) - n2 * mean(sc * n2))
+    gs_low = gs.astype(BF)
+    R.xgs[mine, :] = gs_low
+    share("gs", R.xgs)
+    R.sm[5:6, :] = colsum(gs_low.astype(F32))
+    pass_on("first", R.xfirst)
+    for k in (2, 3, 1, 0):
+        cols = ds(rk[k] * D, D)
+        gi = (dot(gs_low, R.w2[cols, :], 1, 1) * R.gp[k]).astype(BF)
+        if k:
+            R.giout[k] = gi
+            send(R.giout.at[k], R.xgi.at[mine, :], cx["gi"] + k, rdev[k])
+        else:
+            R.xgi[mine, :] = gi
+        R.sm[pl.ds(8 + rk[k], 1), :] = colsum(gi.astype(F32))
+        gs = gs + dot(gi, R.w1[:, cols], 1, 1)
+    R.sm[3:4, :] = colsum(gs * n1)
+    R.sm[4:5, :] = colsum(gs)
+    sc = gs * small(3)
+    gfi = inv1 * (sc - mean(sc) - n1 * mean(sc * n1))
+    R.gfi[...] = gfi
+    gb = gfi.astype(BF)
+    R.xgb[mine, :] = gb
+    share("gb", R.xgb)
+    R.sm[2:3, :] = colsum(gb.astype(F32))
+    ga = dot(gb, R.wo[...], 1, 1).astype(BF)
+    for j in range(4):
+        R.gaout[j] = ga[:, 192 * j:192 * j + 192]
+    cg = chan(4)
+    for k in (2, 1, 3):
+        send(R.gaout.at[zk[k]], R.gag.at[z], cg + k, zdev[k])
+    R.gag[z] = R.gaout[z]
+    pass_on("gs", R.xgs)
+
+    halves = {
+        "2": lambda r, yy: R.G2.at[ds(r * 768, 768), ds(yy * 384, 384)],
+        "1": lambda r, yy: R.G1.at[:, ds(r * 768 + yy * 384, 384)],
+        "o": lambda r, yy: R.Go.at[ds(r * 192, 192), ds(yy * 384, 384)],
+        "q": lambda r, yy: R.Gq.at[:, ds((r % 2) * 384 + (r // 2) * 192 + yy * 96, 96), :],
+        "t": lambda r, yy: R.Gt.at[ds((r % 2) * 256 + (r // 2) * 128, 128), ds(yy * 384, 384)],
+    }
+    pieces = {
+        "2": lambda zz: R.G2.at[ds(row * 768 + zz * 192, 192), ds(y * 384, 384)],
+        "1": lambda zz: R.G1.at[ds(zz * 192, 192), ds(row * 768 + y * 384, 384)],
+        "o": lambda zz: R.Go.at[ds(row * 192 + zz * 48, 48), ds(y * 384, 384)],
+        "q": lambda zz: R.Gq.at[zz, ds(c * 384 + x * 192 + y * 96, 96), :],
+        "t": lambda zz: R.Gt.at[ds(c * 256 + x * 128 + zz * 32, 32), ds(y * 384, 384)],
+    }
+    cs = {n: chan(15) for n in "21oqt"}
+
+    def stage1(n, lhs, rhs, rows):
+        acc, ys, yr = getattr(R, "ac" + n), getattr(R, "ys" + n), getattr(R, "yr" + n)
+        step = min(rows, 256)
+
+        def other(i, _):
+            m = ds(i * step, step)
+            ys[m, :] = dot(lhs[:, m] if rows > step else lhs[...], rhs[:, ds((1 - y) * 384, 384)], 0, 0).astype(BF)
+            return 0
+
+        lax.fori_loop(0, rows // step, other, 0)
+        send(ys, yr, cs[n], ydev)
+
+        def same(i, _):
+            m = ds(i * step, step)
+            acc[m, :] = dot(lhs[:, m] if rows > step else lhs[...], rhs[:, ds(y * 384, 384)], 0, 0)
+            return 0
+
+        lax.fori_loop(0, rows // step, same, 0)
+
+    def stage2(n, rows):
+        acc, zs, yr, zr = (getattr(R, a + n) for a in ("ac", "zs", "yr", "zr"))
+        recv(yr, cs[n])
+        q = rows // 4
+        for k in (2, 1, 3, 0):
+            m = ds(zk[k] * q, q)
+            v = acc[m, :] + yr[m, :].astype(F32)
+            if k:
+                zs[m, :] = v.astype(BF)
+                send(zs.at[m, :], zr.at[k], cs[n] + k, zdev[k])
+            else:
+                acc[m, :] = v
+
+    def stage3(n, rows):
+        acc, zr, fin = (getattr(R, a + n) for a in ("ac", "zr", "fin"))
+        q = rows // 4
+        v = acc[ds(z * q, q), :]
+        for k in (1, 2, 3):
+            recv(zr.at[k], cs[n] + k)
+            v = v + zr[k].astype(F32)
+        fin[...] = v.astype(BF)
+        gatherA(n, fin)
+
+    def gatherA(n, fin):
+        for k in (2, 1, 3):
+            send(fin, pieces[n](z), cs[n] + 3 + k, zdev[k])
+        i = "21oqt".index(n)
+        cp = pltpu.make_async_copy(fin, pieces[n](z), R.wsem.at[8 + i])
+        cp.start()
+        loads["fin" + n] = cp
+
+    def gatherB(n):
+        for k in (1, 2, 3):
+            recv(pieces[n](zb[k]), cs[n] + 3 + k)
+        loads["fin" + n].wait()
+        h = halves[n](row, y)
+        send(h, h, cs[n] + 7, ydev)
+        send(h, h, cs[n] + 8, rdev[2])
+        send(h, h, cs[n] + 9, rdev[1])
+
+    def gatherC(n):
+        h = halves[n](row, 1 - y)
+        recv(h, cs[n] + 7)
+        send(h, h, cs[n] + 10, rdev[2])
+        send(h, h, cs[n] + 11, rdev[1])
+
+    def gatherD(n):
+        h = halves[n](rk[2], y)
+        recv(h, cs[n] + 8)
+        send(h, h, cs[n] + 12, rdev[1])
+
+    def gatherE(n):
+        h = halves[n](rk[2], 1 - y)
+        recv(h, cs[n] + 10)
+        send(h, h, cs[n] + 13, rdev[1])
+
+    def gatherF(n):
+        recv(halves[n](rk[1], y), cs[n] + 9)
+        recv(halves[n](rk[1], 1 - y), cs[n] + 11)
+        recv(halves[n](rk[3], y), cs[n] + 12)
+        recv(halves[n](rk[3], 1 - y), cs[n] + 13)
+
+    def ready(n, ref, forwarded):
+        for k in ((1, 3) if forwarded else (1, 2, 3)):
+            recv(ref.at[rows_at(k), :], cx[n] + k)
+
+    def backward(h):
+        def part(j, _):
+            qs = ds(j * 256, 256)
+            gah = R.ga3[h, qs, :]
+            low = R.pt[h, :, qs]
+            p = low.astype(F32)
+            pd = p * dot(R.v3[h], gah, 1, 1)
+            gr = (pd - p * colsum(pd)).astype(BF)
+            dk = dot(gr, R.q3[h, qs, :])
+            dv = dot(low, gah)
+            R.dk3[h] = jnp.where(j == 0, dk, R.dk3[h] + dk)
+            R.dv3[h] = jnp.where(j == 0, dv, R.dv3[h] + dv)
+            R.dq3[h, qs, :] = (dot(gr, R.k3[h], 0, 0) * 0.125).astype(BF)
+            return 0
+
+        R.dk3[h] = jnp.zeros((L, HD), F32)
+        R.dv3[h] = jnp.zeros((L, HD), F32)
+        lax.fori_loop(0, 2, part, 0)
+
+    ready("act", R.xact, False)
+    ready("gs", R.xgs, True)
+    stage1("2", R.xact, R.xgs, 768)
+    pass_on("gb", R.xgb)
+    for k in (1, 2, 3):
+        recv(R.gag.at[zb[k]], cg + k)
+    for h in range(3):
+        R.ga3[h] = jnp.concatenate([R.gag[j, :, 64 * h:64 * h + 64] for j in range(4)], axis=0)
+    backward(0)
+    ready("gi", R.xgi, False)
+    ready("first", R.xfirst, True)
+    stage1("1", R.xfirst, R.xgi, 768)
+    stage2("2", 768)
+    backward(1)
+    ready("att", R.xatt, False)
+    ready("gb", R.xgb, True)
+    stage1("o", R.xatt, R.xgb, 192)
+    stage3("2", 768)
+    backward(2)
+    ck = chan(1)
+
+    def heads(ref, rows):
+        return [ref[h, rows, :] for h in range(3)]
+
+    theirs, ours = ds((1 - y) * 512, 512), ds(y * 512, 512)
+    R.kvs[...] = jnp.concatenate(heads(R.dk3, theirs) + heads(R.dv3, theirs), axis=1).astype(BF)
+    send(R.kvs, R.kvr, ck, ydev)
+    stage2("1", 768)
+    gatherB("2")
+    stage2("o", 192)
+    recv(R.kvr, ck)
+    both = jnp.concatenate(heads(R.dk3, ours) + heads(R.dv3, ours), axis=1) + R.kvr[...].astype(F32)
+    R.gqkv[...] = jnp.concatenate(heads(R.dq3, slice(None)) + [both.astype(BF)], axis=1)
+    cd = chan(4)
+    for k in (2, 1, 3):
+        send(R.gqkv.at[ds(zk[k] * T, T), :], R.dqin.at[z], cd + k, zdev[k])
+    R.dqin[z] = R.gqkv[ds(z * T, T), :]
+
+    def qgrad(i, _):
+        m = ds(i * 256, 256)
+        R.qp[m, :] = dot(R.elow[ours, m], R.gqkv[...], 0, 0)
+        return 0
+
+    lax.fori_loop(0, 3, qgrad, 0)
+    cq = cs["q"]
+    R.qs0[...] = R.qp[ds((1 - c) * 384, 384), :].astype(BF)
+    send(R.qs0, R.qr0, cq, rdev[1])
+    stage3("1", 768)
+    stage3("o", 192)
+    gatherC("2")
+    gatherD("2")
+    gatherE("2")
+    recv(R.qr0, cq)
+    base = c * 384
+    R.qs1[...] = (R.qp[ds(base + (1 - x) * 192, 192), :] + R.qr0[ds((1 - x) * 192, 192), :].astype(F32)).astype(BF)
+    send(R.qs1, R.qr1, cq + 1, rdev[2])
+    for k in (1, 2, 3):
+        recv(R.dqin.at[zb[k]], cd + k)
+    gq, gk, gv = (jnp.concatenate([R.dqin[j, :, 192 * i:192 * i + 192] for j in range(4)], axis=1) for i in range(3))
+    R.sm[0:1, :] = colsum(gq.astype(F32))
+    R.sm[1:2, :] = colsum(gv.astype(F32))
+    ge = R.gfi[...] + dot(gq, R.wq[...], 1, 1) + dot(gk, R.wk[...], 1, 1) + dot(gv, R.wv[...], 1, 1)
+    gel = ge.astype(BF)
+    R.gtok[...] = gel
+    R.tp[...] = dot(hot_of(me, 512, 0), gel)
+    R.sm[12:14, :] = dot(hot_of(me, 16, 512), gel)[0:2, :]
+    ctb = cs["t"]
+    csm = chan(6)
+    R.ts0[...] = R.tp[ds((1 - c) * 256, 256), :].astype(BF)
+    send(R.ts0, R.tr0, ctb, rdev[1])
+    R.sms[0] = R.sm[...]
+    send(R.sms.at[0], R.smr.at[0], csm, rdev[1])
+    recv(R.qr1, cq + 1)
+    base = c * 384 + x * 192
+    far, near = (1 - y) * 96, y * 96
+
+    def qsum(o):
+        return (R.qp[ds(base + o, 96), :] + R.qr0[ds(x * 192 + o, 96), :].astype(F32)
+                + R.qr1[ds(o, 96), :].astype(F32))
+
+    R.qs2[...] = qsum(far).astype(BF)
+    send(R.qs2, R.qr2, cq + 2, ydev)
+    recv(R.tr0, ctb)
+    R.ts1[...] = (R.tp[ds(c * 256 + (1 - x) * 128, 128), :] + R.tr0[ds((1 - x) * 128, 128), :].astype(F32)).astype(BF)
+    send(R.ts1, R.tr1, ctb + 1, rdev[2])
+    recv(R.smr.at[0], csm)
+    R.sms[1] = R.sms[0] + R.smr[0]
+    send(R.sms.at[1], R.smr.at[1], csm + 1, rdev[2])
+    recv(R.qr2, cq + 2)
+    R.finq[...] = (qsum(near) + R.qr2[...].astype(F32)).astype(BF)
+    gatherA("q", R.finq)
+    gatherB("1")
+    gatherB("o")
+    recv(R.tr1, ctb + 1)
+
+    def tsum(lanes):
+        return (R.tp[ds(c * 256 + x * 128, 128), lanes] + R.tr0[ds(x * 128, 128), lanes].astype(F32)
+                + R.tr1[:, lanes].astype(F32))
+
+    R.ts2[...] = tsum(ds((1 - y) * 384, 384)).astype(BF)
+    send(R.ts2, R.tr2, ctb + 2, ydev)
+    recv(R.smr.at[1], csm + 1)
+    R.sms[2] = R.sms[1] + R.smr[1]
+    send(R.sms.at[2], R.smr.at[2], csm + 2, ydev)
+    gatherC("1")
+    gatherC("o")
+    gatherB("q")
+    recv(R.tr2, ctb + 2)
+    tv = tsum(ds(y * 384, 384)) + R.tr2[...].astype(F32)
+    R.ts3[...] = tv.astype(BF)
+    ctz = chan(4)
+    for k in (2, 1, 3):
+        send(R.ts3.at[ds(zk[k] * 32, 32), :], R.tr3.at[k], ctz + k, zdev[k])
+    recv(R.smr.at[2], csm + 2)
+    R.sms[3] = R.sms[2] + R.smr[2]
+    for k in (2, 1, 3):
+        send(R.sms.at[3], R.smr.at[2 + k], csm + 2 + k, zdev[k])
+    tfin = jnp.zeros((32, 384), F32)
+    R.tp[0:128, 0:384] = tv
+    tfin = R.tp[ds(z * 32, 32), 0:384]
+    for k in (1, 2, 3):
+        recv(R.tr3.at[k], ctz + k)
+        tfin = tfin + R.tr3[k].astype(F32)
+    R.fint[...] = tfin.astype(BF)
+    gatherA("t", R.fint)
+    gatherC("q")
+    gatherB("t")
+    gatherC("t")
+    total = R.sms[3]
+    for k in (1, 2, 3):
+        recv(R.smr.at[2 + k], csm + 2 + k)
+        total = total + R.smr[2 + k]
+    R.Gs[...] = total
+    for n in "1oqt":
+        gatherD(n)
+        gatherE(n)
+    for n in "21oqt":
+        gatherF(n)
+    for cp in pending:
+        cp.wait_send()
+
+
+def mega(*args):
+    S = jax.ShapeDtypeStruct
+    any_, vm = pl.BlockSpec(memory_space=pl.ANY), pl.BlockSpec(memory_space=VMEM)
+    return pl.pallas_call(
+        kernel,
+        out_shape=(S((T, D), BF), S((T, D), BF), S((F, D), BF), S((D, F), BF), S((D, D), BF), S((4, D, 576), BF),
+                   S((512, D), BF), S((16, D), F32)),
+        in_specs=[vm] * 6 + [any_] * 6,
+        out_specs=(vm, vm) + (any_,) * 5 + (vm,),
+        scratch_shapes=list(scratch().values()),
+        compiler_params=pltpu.CompilerParams(collective_id=0, has_side_effects=True, vmem_limit_bytes=63 << 20),
+    )(*args)
+
+
+def fast_device(tokens, cotangent, segment_ids, restarts, position_table, query_weight, query_bias, key_weight,
+                value_weight, value_bias, out_weight, out_bias, first_gain, first_shift, inner_weight, inner_bias,
+                outer_weight, outer_bias, second_gain, second_shift):
+    vectors = (query_bias, value_bias, out_bias, first_gain, first_shift, outer_bias, second_gain, second_shift)
+    small = jnp.concatenate([v.astype(F32) for v in vectors] + [inner_bias.astype(F32), jnp.zeros((4 * D,), F32)])
+    layer, gtok, g2, g1, go, gq, gt, gs = mega(
+        tokens[0], cotangent[0], segment_ids, restarts, position_table, small.reshape(16, D), query_weight,
+        key_weight, value_weight, out_weight, inner_weight, outer_weight)
+
+    def heads(i):
+        return jnp.swapaxes(gq[:, :, 192 * i:192 * i + 192], 0, 1).reshape(D, D).astype(F32)
+
+    table = jnp.concatenate([gt.astype(F32), gs[12:14]], axis=0)
+    return (layer[None], gtok[None], table, heads(0), gs[0], heads(1), heads(2), gs[1], go.astype(F32), gs[2], gs[3],
+            gs[4], g1.astype(F32), gs[8:12].reshape(F), g2.astype(F32), gs[5], gs[6], gs[7])
+
 
 HEADS = 12
 
@@ -433,6 +1069,7 @@
         P(),
         P(),
     )
+    body = fast_device if mesh.shape["seq"] == 8 and mesh.shape["rows"] == 4 else per_device
     return jax.shard_map(
-        per_device, mesh=mesh, in_specs=in_specs, out_specs=out_specs, check_vma=False
-    )
+        body, mesh=mesh, in_specs=in_specs, out_specs=out_specs, check_vma=False
+    )

time: 1460 us -> 284 us (0.19)
  waiting for transfers between devices: 1230 us -> 0 us
  Pallas kernels: 0 us -> 234 us
  blocking collectives: 72 us -> 0 us
  matrix products: 67.5 us -> 0 us
  other arithmetic: 43.3 us -> 26 us
    reduce_scatter x8 -> x0, waiting for transfers between devices: 728 us -> none  [the longest x1 165 us: per_device(): lax.psum_scatter(grad_winner, 'seq', scatter_dimension=0, tiled=True)]
    all_gather x8 -> x0, waiting for transfers between devices: 323 us -> none  [the longest x1 78.1 us: per_device(): lax.all_gather(pieces[4].astype(jnp.bfloat16), 'seq', axis=0, tiled=True)]
    pallas_call x0 -> x1, Pallas kernels: none -> 234 us  [mega(): pl.pallas_call(kernel, out_shape=(S((T, D), BF), S((T, D), BF), S((F, D),...]
    psum x2 -> x0, waiting for transfers between devices: 177 us -> none  [the longest x1 129 us: per_device(): lax.psum((grad_table, grad_bquery, grad_bvalue, grad_bout, grad_gfirst, g...]
    dot_general x26 -> x0, matrix products: 67.5 us -> none  [the longest x6 20 us: outer_sum(): lax.dot_general(left, right, (((0,), (0,)), ((), ())), preferred_element_...]
    psum x1 -> x0, blocking collectives: 41.3 us -> none  [per_device(): lax.psum((grad_table, grad_bquery, grad_bvalue, grad_bout, grad_gfirst, g...]
    convert_element_type x21 -> x5, other arithmetic: 36.5 us -> 18.5 us  [the longest x1 7.52 us: fast_device(): g1.astype(F32)]
    all_gather x1 -> x0, blocking collectives: 17.7 us -> none  [per_device(): lax.all_gather(segment_ids, 'seq', axis=1, tiled=True)]
  transfers between devices with their start and end apart: 18 -> 0, of which waited for: 17 -> 0; matrix products, arithmetic and copies ran while one was open for 5% -> 0% of each run, Pallas kernels for 0% -> 0%
where the time goes in v1:
time: 284 us; the launch traced here: 283 us
  Pallas kernels  234 us (82%)
  other arithmetic  26 us (9%)
  local copies, waits for them, and re-layouts  22.1 us (8%)
    pallas_call x1, Pallas kernels, mega(): pl.pallas_call(kernel, out_shape=(S((T, D), BF), S((T, D), BF), S((F, D),...  234 us
    unnamed x19, local copies, waits for them, and re-layouts  10.6 us
    convert_element_type x3, local copies, waits for them, and re-layouts, heads(): jnp.swapaxes(gq[:, :, 192 * i:192 * i + 192], 0, 1).reshape(D, D)  8.85 us
    convert_element_type x1, other arithmetic, fast_device(): g1.astype(F32)  7.52 us
    unnamed x11, other arithmetic  6.2 us

profile of v1, /device:TPU:0, one launch (start us, length us, event | category | flops | bytes accessed | tf_op | source)
XLA Modules:
  0.0 282.6 jit_solution(2788870369003988330)
XLA Ops:
  0.7 0.7 constant_dynamic-update-slice_fusion.7
  1.4 0.7 constant_dynamic-update-slice_fusion.6
  2.0 0.7 constant_dynamic-update-slice_fusion.5
  2.7 0.7 constant_dynamic-update-slice_fusion.4
  3.4 0.7 constant_dynamic-update-slice_fusion.3
  4.1 0.7 constant_dynamic-update-slice_fusion.2
  4.8 0.7 constant_dynamic-update-slice_fusion.1
  5.5 0.7 constant_dynamic-update-slice_fusion
  6.2 0.7 convert_dynamic-update-slice_fusion
  6.9 0.6 reshape.51.refs_5_
  7.5 233.8 %shard_map.331 = (bf16[128,768]{1,0:T(8,128)(2,1)}, bf16[128,768]{1,0:T(8,128)(2,1)}, bf16[3072,768]{1,0:T(8,128)(2,1)}, bf16[768,3072]{1,0:T(8,128)(2,1)}, bf16...) custom-call(bf16[128,768]{1,0:T(8,128)(2,1)} %bitcast.18, ...), custom_call_target="tpu_custom_call" | custom-call | tf_op jit(solution)/shard_map/pallas_call | solution.py:616
  241.3 0.7 slice.39
  242.1 1.4 convert_element_type.75
  243.4 1.3 pad_maximum_fusion
  244.7 0.0 copy-done.4
  244.7 0.7 slice_reduce_fusion
  245.4 0.0 copy-done
  245.4 3.6 %convert_bitcast_fusion = (f32[768,4,192]{2,0,1:T(8,128)S(1)}, f32[768,4,192]{2,0,1:T(8,128)}, f32[768,4,192]{2,0,1:T(8,128)}) fusion(bf16[4,768,576]{2,1,0:T(8,128)(2,1)S(1)} %copy-done), kind=kLoop, calls=%fused_computation | loop fusion | flops 1769472 | bytes 10616832 | tf_op jit(solution)/shard_map/convert_element_type | solution.py:637
  248.9 3.3 %copy.38 = f32[768,4,192]{0,2,1:T(8,128)} copy(f32[768,4,192]{2,0,1:T(8,128)} %get-tuple-element.62) | data formatting | bytes 4718592 | tf_op jit(solution)/shard_map/convert_element_type | solution.py:637
  252.3 3.0 %copy.41 = f32[768,768]{1,0:T(8,128)} copy(f32[768,768]{0,1:T(8,128)} %bitcast.13) | data formatting | bytes 4718592
  255.3 3.3 %copy.39 = f32[768,4,192]{0,2,1:T(8,128)} copy(f32[768,4,192]{2,0,1:T(8,128)} %get-tuple-element.61) | data formatting | bytes 4718592 | tf_op jit(solution)/shard_map/convert_element_type | solution.py:637
  258.7 3.0 %copy.42 = f32[768,768]{1,0:T(8,128)} copy(f32[768,768]{0,1:T(8,128)} %bitcast.14) | data formatting | bytes 4718592
  261.7 2.2 copy.40
  263.9 3.1 %copy.43 = f32[768,768]{1,0:T(8,128)} copy(f32[768,768]{0,1:T(8,128)} %bitcast.15) | data formatting | bytes 4718592
  267.0 0.6 reshape.52
  267.6 7.5 %convert_element_type.86 = f32[768,3072]{1,0:T(8,128)} convert(bf16[768,3072]{1,0:T(8,128)(2,1)} %get-tuple-element.32) | non-fusion elementwise | flops 2359296 | bytes 14155776 | tf_op jit(solution)/shard_map/convert_element_type | solution.py:641
  275.1 0.0 slice-done
  275.1 0.0 slice-done.1
  275.1 4.5 %convert_element_type.87 = f32[3072,768]{1,0:T(8,128)} convert(bf16[3072,768]{1,0:T(8,128)(2,1)S(1)} %bitcast.17) | non-fusion elementwise | flops 2359296 | bytes 14155776 | tf_op jit(solution)/shard_map/convert_element_type | solution.py:641
  279.6 1.6 convert_element_type.85
  281.2 0.7 copy.56
  281.9 0.7 copy.57
  (14 shorter events, 0.0 us)
Async XLA Ops:
  242.0 2.7 copy-start.4
  242.1 3.3 %copy-start = (bf16[4,768,576]{2,1,0:T(8,128)(2,1)S(1)}, bf16[4,768,576]{2,1,0:T(8,128)(2,1)}, u32[]{:S(2)}) copy-start(bf16[4,768,576]{2,1,0:T(8,128)(2,1)} %get-tuple-element.30) | copy-start | bytes 10616836
  263.9 11.2 %slice-start = ((s8[4718592]{0:T(1024)(128)(4,1)}), s8[524288]{0:T(1024)(128)(4,1)S(1)}, s32[]{:S(2)}) async-start(s8[4718592]{0:T(1024)(128)(4,1)} %bitcast.16), calls=%async_computation | async-start | bytes 1048576
  267.6 7.5 %slice-start.1 = ((s8[4718592]{0:T(1024)(128)(4,1)}), s8[4194304]{0:T(1024)(128)(4,1)S(1)}, s32[]{:S(2)}) async-start(s8[4718592]{0:T(1024)(128)(4,1)} %bitcast.16), calls=%async_computation.1 | async-start | bytes 8388608
  275.1 4.5 %copy-start.1 = (bf16[768,768]{1,0:T(8,128)(2,1)S(1)}, bf16[768,768]{1,0:T(8,128)(2,1)}, u32[]{:S(2)}) copy-start(bf16[768,768]{1,0:T(8,128)(2,1)} %get-tuple-element.31) | copy-start | bytes 3538948
  279.6 1.6 copy-start.3
  279.6 2.3 copy-start.2

commit v2 on v0

--- a/solution.py
+++ b/solution.py
@@ -1,9 +1,742 @@
 from functools import partial
+from types import SimpleNamespace
 
 import jax
 import jax.numpy as jnp
 from jax import lax
+from jax.experimental import pallas as pl
+from jax.experimental.pallas import tpu as pltpu
 from jax.sharding import PartitionSpec as P
+
+MESH = pl.DeviceIdType.MESH
+VMEM = pltpu.VMEM
+BF, F32, I32 = jnp.bfloat16, jnp.float32, jnp.int32
+T, D, F, L, HD = 128, 768, 3072, 1024, 64
+EPS = 1e-5
+CHANNELS = 220
+ROWS_OF = {"2a": 384, "2b": 384, "1a": 384, "1b": 384, "o": 192}
+STREAMS = tuple(ROWS_OF) + ("q", "t")
+ORDER = (
+    "gs", "12a", "12b", "in", "h0", "11a", "11b", "gb", "h1", "22a", "1o", "h2", "kv", "21a", "22b", "21b", "32a", "vk", "q0",
+    "2o", "31a", "q1", "32b", "B2a", "31b", "3o", "B1a", "q2", "en", "C2a", "C1a", "D2a", "D1a", "B2b", "B1b", "t1", "q3",
+    "Bo", "C2b", "C1b", "E2a", "E1a", "t2", "Co", "Bq", "t3", "D2b", "D1b", "Do", "t4", "Cq", "E2b", "E1b", "Eo", "Bt", "Dq",
+    "Ct", "Eq", "Dt", "Et", "F2a", "F1a", "F2b", "F1b", "Fo", "as", "Ft")
+
+
+def dot(a, b, ca=1, cb=0):
+    return lax.dot_general(a, b, (((ca,), (cb,)), ((), ())), preferred_element_type=F32)
+
+
+def ds(start, size, step=None):
+    return pl.ds(pl.multiple_of(start, step or size), size)
+
+
+def scratch():
+    s = {}
+    s["tok"] = VMEM((8, T, D), BF)
+    s["meta"] = VMEM((8, 8, T), I32)
+    s["tail"] = VMEM((16, D), BF)
+    s["table"] = VMEM((514, D), BF)
+    s["cot"] = VMEM((T, D), BF)
+    s["pos"] = VMEM((8, 8, T), I32)
+    s["segc"] = VMEM((L, T), F32)
+    s["segq"] = VMEM((2, 8, 256), F32)
+    s["elow"] = VMEM((4 * T, D), BF)
+    s["q3"] = VMEM((3, 512, HD), BF)
+    s["k3"] = VMEM((3, L, HD), BF)
+    s["v3"] = VMEM((3, L, HD), BF)
+    s["pt"] = VMEM((3, L, 512), BF)
+    s["stat"] = VMEM((3, 2, 8, 256), F32)
+    s["half"] = VMEM((3, HD, 512), F32)
+    s["attcat"] = VMEM((4, 192, T), BF)
+    s["attg"] = VMEM((4, 192, T), BF)
+    s["own"] = VMEM((T, D), F32)
+    for n in ("first", "act", "gs", "gi", "gb"):
+        s["x" + n] = VMEM((4 * T, D), BF)
+    s["xatt"] = VMEM((192, 4 * T), BF)
+    s["gp"] = VMEM((4 * T, D), F32)
+    s["gaout"] = VMEM((4, T, 192), BF)
+    s["gag"] = VMEM((4, T, 192), BF)
+    s["ga3"] = VMEM((3, 512, HD), BF)
+    s["dk"] = VMEM((L, HD), F32)
+    s["dv"] = VMEM((L, HD), F32)
+    s["kvo"] = VMEM((512, 384), F32)
+    s["kvs"] = VMEM((512, 384), BF)
+    s["kvr"] = VMEM((512, 384), BF)
+    s["gqkv"] = VMEM((512, 576), BF)
+    s["dqin"] = VMEM((4, T, 576), BF)
+    for n, m in ROWS_OF.items():
+        s["bs" + n] = VMEM((m, 384), BF)
+        s["br" + n] = VMEM((m, 384), BF)
+        s["ac" + n] = VMEM((m, 384), F32)
+        s["zr" + n] = VMEM((3, m // 4, 384), BF)
+    s["qp"] = VMEM((384, 576), F32)
+    for i, m in ((0, 384), (1, 192), (2, 96)):
+        s["qs%d" % i] = VMEM((m, 576), BF)
+        s["qr%d" % i] = VMEM((m, 576), BF)
+    s["Gq"] = VMEM((4, D, 576), BF)
+    for i, m in ((0, 256), (1, 128)):
+        s["ts%d" % i] = VMEM((m, D), BF)
+        s["tr%d" % i] = VMEM((m, D), BF)
+    s["ts2"] = VMEM((128, 384), BF)
+    s["tr2"] = VMEM((128, 384), BF)
+    s["ts3"] = VMEM((128, 384), BF)
+    s["tr3"] = VMEM((4, 32, 384), BF)
+    s["sm"] = VMEM((16, D), F32)
+    s["sms"] = VMEM((4, 16, D), F32)
+    s["smr"] = VMEM((6, 16, D), F32)
+    s["wsem"] = pltpu.SemaphoreType.DMA((9,))
+    s["ss"] = pltpu.SemaphoreType.DMA((CHANNELS,))
+    s["rs"] = pltpu.SemaphoreType.DMA((CHANNELS,))
+    return s
+
+
+INPUTS = ("tokens", "hcot", "segs", "rests", "htable", "small", "hq", "hk", "hv", "ho", "h1", "h2")
+OUTPUTS = ("layer", "gtok", "G2", "G1", "Go", "Gwq", "Gwk", "Gwv", "Gt", "Gs")
+
+
+def kernel(*refs):
+    names = INPUTS + OUTPUTS + tuple(scratch())
+    R = SimpleNamespace(**dict(zip(names, refs, strict=True)))
+    seq, row = lax.axis_index("seq"), lax.axis_index("rows")
+    z, y, x, c = seq // 2, seq % 2, row // 2, row % 2
+    zk = [(z + k) % 4 for k in range(4)]
+    zb = [(z + 4 - k) % 4 for k in range(4)]
+    rk = [row, x * 2 + (1 - c), (1 - x) * 2 + c, (1 - x) * 2 + (1 - c)]
+    zdev = [(zk[k] * 2 + y, row) for k in range(4)]
+    ydev = (z * 2 + (1 - y), row)
+    rdev = [(seq, rk[k]) for k in range(4)]
+    counter = [0]
+    pending = []
+
+    def chan(n=1):
+        counter[0] += n
+        assert counter[0] <= CHANNELS
+        return counter[0] - n
+
+    def copy(src, dst, i, dev):
+        return pltpu.make_async_remote_copy(src, dst, R.ss.at[i], R.rs.at[i], device_id=dev, device_id_type=MESH)
+
+    def send(src, dst, i, dev):
+        cp = copy(src, dst, i, dev)
+        cp.start()
+        pending.append(cp)
+
+    def recv(dst, i):
+        copy(dst, dst, i, ydev).wait_recv()
+
+    yxdev = (z * 2 + (1 - y), x * 2 + (1 - c))
+    gx = SimpleNamespace(w=[row, *rk[1:]], dev=rdev, b=y, bdev=ydev)
+    wy = y * 2 + c
+    gy = SimpleNamespace(w=[wy, y * 2 + (1 - c), (1 - y) * 2 + c, (1 - y) * 2 + (1 - c)],
+                         dev=[(seq, row), rdev[1], ydev, yxdev], b=x, bdev=rdev[2])
+    group = {n: gy if n[0] in "1o" else gx for n in STREAMS}
+    group.update(first=gy, gi=gy, att=gy, gb=gy, act=gx, gs=gx)
+
+    loads = {}
+    weights = (("n", R.tokens, R.tok.at[y * 4 + z]), ("t", R.htable, R.table), ("k", R.hk, R.Gwk), ("v", R.hv, R.Gwv), ("q", R.hq, R.Gwq), ("c", R.hcot, R.cot), ("o", R.ho, R.Go), ("1", R.h1, R.G1), ("2", R.h2, R.G2))
+
+    def load(i):
+        n, src, dst = weights[i]
+        loads[n] = pltpu.make_async_copy(src, dst, R.wsem.at[i])
+        loads[n].start()
+
+    for i in range(5):
+        load(i)
+
+    me = y * 4 + z
+    R.meta[me] = jnp.zeros((8, T), I32)
+    R.meta[me, 0:1, :] = R.rests[...]
+    R.meta[me, 1:2, :] = R.segs[...]
+    seqpeers = [zdev[1], zdev[2], zdev[3]] + [(zk[k] * 2 + (1 - y), row) for k in range(4)]
+    peers = seqpeers + rdev[1:] + [yxdev]
+    bar = pltpu.get_barrier_semaphore()
+    for p in peers:
+        pl.semaphore_signal(bar, inc=1, device_id=p, device_id_type=MESH)
+    pl.semaphore_wait(bar, len(peers))
+    loads["n"].wait()
+    cm = chan(7)
+    metas = []
+    for i, dev in enumerate(seqpeers):
+        cp = copy(R.meta.at[me], R.meta.at[me], cm + i, dev)
+        cp.start()
+        metas.append(cp)
+    ct = chan(8)
+    tokens_out = []
+
+    def forward(b, i, dev):
+        tokens_out.append(copy(R.tok.at[b], R.tok.at[b], i, dev))
+        tokens_out[-1].start()
+
+    for k in (1, 2, 3):
+        forward(me, ct + k, zdev[k])
+    forward(me, ct + 4, ydev)
+    for i in range(5, 9):
+        load(i)
+    loads["t"].wait()
+    R.tail[...] = jnp.zeros((16, D), BF)
+    R.tail[0:2, :] = R.table[512:514, :]
+    for cp in metas:
+        cp.wait()
+    lane = lax.broadcasted_iota(I32, (8, T), 1)
+    spot = lax.broadcasted_iota(I32, (8, T), 0) * T + lane
+    block_of = [(s % 2) * 4 + s // 2 for s in range(8)]
+    flags = jnp.concatenate([R.meta[b, 0:1, :] for b in block_of], axis=0)
+    mk = jnp.where(flags == 1, spot, -1)
+    k = 1
+    while k < T:
+        mk = jnp.where(lane >= k, jnp.maximum(mk, pltpu.roll(mk, k, axis=1)), mk)
+        k *= 2
+    tot = jnp.max(mk, axis=1, keepdims=True)
+    carry = jnp.full((1, 1), -1, I32)
+    for s, b in enumerate(block_of):
+        late = jnp.maximum(mk[s:s + 1, :], carry)
+        R.pos[b, 0:1, :] = spot[s:s + 1, :] - late + 2
+        carry = jnp.maximum(carry, tot[s:s + 1, :])
+    for b in range(8):
+        R.segc[b * T:(b + 1) * T, :] = jnp.broadcast_to(R.meta[b, 1:2, :], (T, T)).astype(F32).T
+    for j in range(2):
+        R.segq[j, 0:1, :] = jnp.concatenate([R.meta[y * 4 + 2 * j + i, 1:2, :] for i in range(2)], axis=1).astype(F32)
+
+    off = pl.multiple_of(128 * ((3 * z) // 2), 128)
+    odd = (z % 2) == 1
+
+    def window(v):
+        return jnp.where(odd, v[:, 64:256], v[:, 0:192])
+
+    bq = R.small[0:1, pl.ds(off, 256)]
+    bv = R.small[1:2, pl.ds(off, 256)]
+    for n in "kvq":
+        loads[n].wait()
+
+    def hot_of(b, size, start):
+        return (lax.broadcasted_iota(I32, (size, T), 0) + start == R.pos[b, 0:1, :]).astype(BF)
+
+    def block(b, with_q):
+        e = dot(hot_of(b, 512, 0), R.table[0:512, :], 0, 0) + dot(hot_of(b, 16, 512), R.tail[...], 0, 0)
+        e = e + R.tok[b].astype(F32)
+        el = e.astype(BF)
+        here = ds(b * T, T)
+        kk = window(dot(el, R.Gwk[:, pl.ds(off, 256)])).astype(BF)
+        vv = window(dot(el, R.Gwv[:, pl.ds(off, 256)]) + bv).astype(BF)
+        for h in range(3):
+            R.k3[h, here, :] = kk[:, 64 * h:64 * h + 64]
+            R.v3[h, here, :] = vv[:, 64 * h:64 * h + 64]
+        if with_q:
+            qq = (window(dot(el, R.Gwq[:, pl.ds(off, 256)]) + bq) * 0.125).astype(BF)
+            there = ds((b - y * 4) * T, T)
+            R.elow[there, :] = el
+            for h in range(3):
+                R.q3[h, there, :] = qq[:, 64 * h:64 * h + 64]
+        return e
+
+    R.own[...] = block(me, True)
+
+    for k in (1, 2, 3):
+        b = y * 4 + zb[k]
+        recv(R.tok.at[b], ct + k)
+        forward(b, ct + 4 + k, ydev)
+        block(b, True)
+
+    def scores(h, j, parity):
+        rows, qs = ds(parity * 512, 512), ds(j * 256, 256)
+        s = dot(R.k3[h, rows, :], R.q3[h, qs, :], 1, 1)
+        sc = R.segc[rows, :]
+        s = jnp.where(jnp.concatenate([sc, sc], axis=1) == R.segq[j, 0:1, :], s, -1e30)
+        top = jnp.max(s, axis=0, keepdims=True)
+        p = jnp.exp(s - top)
+        low = p.astype(BF)
+        R.pt[h, rows, qs] = low
+        return top, jnp.sum(p, axis=0, keepdims=True), dot(R.v3[h, rows, :], low, 0, 0)
+
+    def attend_near(i, _):
+        h, j = i // 2, i % 2
+        top, den, acc = scores(h, j, y)
+        R.stat[h, j, 2:3, :] = top
+        R.stat[h, j, 3:4, :] = den
+        R.half[h, :, ds(j * 256, 256)] = acc
+        return 0
+
+    def attend_far(i, _):
+        h, j = i // 2, i % 2
+        top, den, acc = scores(h, j, 1 - y)
+        top0 = R.stat[h, j, 2:3, :]
+        most = jnp.maximum(top, top0)
+        f, f0 = jnp.exp(top - most), jnp.exp(top0 - most)
+        inv = 1.0 / (den * f + R.stat[h, j, 3:4, :] * f0)
+        f, f0 = f * inv, f0 * inv
+        R.stat[h, j, pl.ds(y, 1), :] = f0
+        R.stat[h, j, pl.ds(1 - y, 1), :] = f
+        qs = ds(j * 256, 256)
+        R.half[h, :, qs] = acc * f + R.half[h, :, qs] * f0
+        return 0
+
+    lax.fori_loop(0, 6, attend_near, 0)
+    for k in (0, 1, 2, 3):
+        b = (1 - y) * 4 + zb[k]
+        recv(R.tok.at[b], ct + 4 + k)
+        block(b, False)
+    lax.fori_loop(0, 6, attend_far, 0)
+    for j in range(4):
+        R.attcat[j] = jnp.concatenate([R.half[h, :, j * T:(j + 1) * T] for h in range(3)], axis=0).astype(BF)
+    ca = chan(4)
+    for k in (2, 1, 3):
+        send(R.attcat.at[zk[k]], R.attg.at[z], ca + k, zdev[k])
+    R.attg[z] = R.attcat[z]
+    for n in "co12":
+        loads[n].wait()
+    for cp in tokens_out:
+        cp.wait_send()
+    for k in (1, 2, 3):
+        recv(R.attg.at[zb[k]], ca + k)
+
+    def slot(n, k):
+        return ds(group[n].w[k] * T, T)
+
+    def small(i):
+        return R.small[i:i + 1, :]
+
+    def colsum(v):
+        return jnp.sum(v, axis=0, keepdims=True)
+
+    def mean(v):
+        return jnp.mean(v, axis=-1, keepdims=True)
+
+    R.sm[...] = jnp.zeros((16, D), F32)
+    cx = {n: chan(4) for n in ("first", "act", "att", "gs", "gi", "gb")}
+
+    def share(n, ref):
+        mine = ref.at[slot(n, 0), :]
+        send(mine, mine, cx[n] + 2, group[n].dev[2])
+        send(mine, mine, cx[n] + 1, group[n].dev[1])
+
+    def pass_on(n, ref):
+        theirs = ref.at[slot(n, 2), :]
+        recv(theirs, cx[n] + 2)
+        send(theirs, theirs, cx[n] + 3, group[n].dev[1])
+
+    u = R.own[...] + dot(jnp.concatenate([R.attg[j] for j in range(4)], axis=0), R.Go[...], 0, 0) + small(2)
+    u = u - mean(u)
+    inv1 = lax.rsqrt(mean(u * u) + EPS)
+    n1 = u * inv1
+    first = n1 * small(3) + small(4)
+    first_low = first.astype(BF)
+    R.xfirst[slot("first", 0), :] = first_low
+    share("first", R.xfirst)
+    second = jnp.zeros((T, D), F32)
+    for k in (2, 3, 1, 0):
+        q = gx.w[k]
+        cols = ds(q * D, D)
+        inner = dot(first_low, R.G1[:, cols]) + R.small[pl.ds(8 + q, 1), :]
+        phi = 0.5 * (1.0 + lax.erf(inner * 0.7071067811865476))
+        R.gp[ds(q * T, T), :] = phi + inner * (0.3989422804014327 * jnp.exp(-0.5 * inner * inner))
+        act = (inner * phi).astype(BF)
+        if k:
+            R.tok[k] = act
+            send(R.tok.at[k], R.xact.at[slot("act", 0), :], cx["act"] + k, gx.dev[k])
+        else:
+            R.xact[slot("act", 0), :] = act
+        second = second + dot(act, R.G2[cols, :])
+    for k in (1, 2, 3):
+        send(R.attg.at[gy.w[k]], R.xatt.at[:, slot("att", 0)], cx["att"] + k, gy.dev[k])
+    R.xatt[:, slot("att", 0)] = R.attg[gy.w[0]]
+    u = first + second + small(5)
+    u = u - mean(u)
+    inv2 = lax.rsqrt(mean(u * u) + EPS)
+    n2 = u * inv2
+    R.layer[...] = (n2 * small(6) + small(7)).astype(BF)
+    g = R.cot[...].astype(F32)
+    R.sm[6:7, :] = colsum(g * n2)
+    R.sm[7:8, :] = colsum(g)
+    sc = g * small(6)
+    gs = inv2 * (sc - mean(sc) - n2 * mean(sc * n2))
+    gs_low = gs.astype(BF)
+    R.xgs[slot("gs", 0), :] = gs_low
+    share("gs", R.xgs)
+    R.sm[5:6, :] = colsum(gs_low.astype(F32))
+    pass_on("first", R.xfirst)
+    for k in (2, 3, 1, 0):
+        q = gy.w[k]
+        cols = ds(q * D, D)
+        gi = (dot(gs_low, R.G2[cols, :], 1, 1) * R.gp[ds(q * T, T), :]).astype(BF)
+        if k:
+            R.tok[4 + k] = gi
+            send(R.tok.at[4 + k], R.xgi.at[slot("gi", 0), :], cx["gi"] + k, gy.dev[k])
+        else:
+            R.xgi[slot("gi", 0), :] = gi
+        R.sm[pl.ds(8 + q, 1), :] = colsum(gi.astype(F32))
+        gs = gs + dot(gi, R.G1[:, cols], 1, 1)
+    R.sm[3:4, :] = colsum(gs * n1)
+    R.sm[4:5, :] = colsum(gs)
+    sc = gs * small(3)
+    gfi = inv1 * (sc - mean(sc) - n1 * mean(sc * n1))
+    R.own[...] = gfi
+    gb = gfi.astype(BF)
+    R.xgb[slot("gb", 0), :] = gb
+    ga = dot(gb, R.Go[...], 1, 1).astype(BF)
+    for j in range(4):
+        R.gaout[j] = ga[:, 192 * j:192 * j + 192]
+    cg = chan(4)
+    for k in (2, 1, 3):
+        send(R.gaout.at[zk[k]], R.gag.at[z], cg + k, zdev[k])
+    R.gag[z] = R.gaout[z]
+    share("gb", R.xgb)
+    R.sm[2:3, :] = colsum(gb.astype(F32))
+
+    def two(h):
+        lo = 384 * h
+        return (lambda w, b: R.G2.at[ds(w * 768 + lo, 384), ds(b * 384, 384)],
+                lambda w, b, zz: R.G2.at[ds(w * 768 + lo + zz * 96, 96), ds(b * 384, 384)])
+
+    def one(h):
+        lo = 384 * h
+        return (lambda w, b: R.G1.at[lo:lo + 384, ds(w * 768 + b * 384, 384)],
+                lambda w, b, zz: R.G1.at[ds(lo + zz * 96, 96), ds(w * 768 + b * 384, 384)])
+
+    regions = {
+        "2a": two(0), "2b": two(1), "1a": one(0), "1b": one(1),
+        "o": (lambda w, b: R.Go.at[ds(w * 192, 192), ds(b * 384, 384)],
+              lambda w, b, zz: R.Go.at[ds(w * 192 + zz * 48, 48), ds(b * 384, 384)]),
+        "q": (lambda w, b: R.Gq.at[:, ds((w % 2) * 384 + (w // 2) * 192 + b * 96, 96), :],
+              lambda w, b, zz: R.Gq.at[zz, ds((w % 2) * 384 + (w // 2) * 192 + b * 96, 96), :]),
+        "t": (lambda w, b: R.Gt.at[ds((w % 2) * 256 + (w // 2) * 128, 128), ds(b * 384, 384)],
+              lambda w, b, zz: R.Gt.at[ds((w % 2) * 256 + (w // 2) * 128 + zz * 32, 32), ds(b * 384, 384)]),
+    }
+    operands = {"2a": (R.xact, 0, R.xgs), "2b": (R.xact, 384, R.xgs), "1a": (R.xfirst, 0, R.xgi), "1b": (R.xfirst, 384, R.xgi)}
+    cs = {n: chan(15) for n in STREAMS}
+    arrived = set()
+
+    def ready(n, ref, forwarded=True):
+        if n not in arrived:
+            arrived.add(n)
+            for k in ((1, 3) if forwarded else (1, 2, 3)):
+                recv(ref.at[:, slot(n, k)] if n == "att" else ref.at[slot(n, k), :], cx[n] + k)
+
+    def stage1(n):
+        acc, bs, br = getattr(R, "ac" + n), getattr(R, "bs" + n), getattr(R, "br" + n)
+        b = group[n].b
+        if n == "o":
+            ready("att", R.xatt, False)
+            ready("gb", R.xgb)
+            bs[...] = dot(R.xatt[...], R.xgb[:, ds((1 - b) * 384, 384)]).astype(BF)
+            send(bs, br, cs[n], group[n].bdev)
+            acc[...] = dot(R.xatt[...], R.xgb[:, ds(b * 384, 384)])
+            return
+        if n[0] == "2":
+            ready("act", R.xact, False)
+            ready("gs", R.xgs)
+        else:
+            ready("gi", R.xgi, False)
+            ready("first", R.xfirst)
+        lhs, lo, rhs = operands[n]
+
+        def other(i, _):
+            bs[ds(i * 128, 128), :] = dot(lhs[:, ds(lo + i * 128, 128)], rhs[:, ds((1 - b) * 384, 384)], 0, 0).astype(BF)
+            return 0
+
+        def same(i, _):
+            acc[ds(i * 128, 128), :] = dot(lhs[:, ds(lo + i * 128, 128)], rhs[:, ds(b * 384, 384)], 0, 0)
+            return 0
+
+        lax.fori_loop(0, 3, other, 0)
+        send(bs, br, cs[n], group[n].bdev)
+        lax.fori_loop(0, 3, same, 0)
+
+    def stage2(n):
+        acc, br, zr = (getattr(R, a + n) for a in ("ac", "br", "zr"))
+        recv(br, cs[n])
+        q = ROWS_OF[n] // 4
+        for k in (2, 1, 3, 0):
+            m = ds(zk[k] * q, q)
+            v = acc[m, :] + br[m, :].astype(F32)
+            if k:
+                br[m, :] = v.astype(BF)
+                send(br.at[m, :], zr.at[k - 1], cs[n] + k, zdev[k])
+            else:
+                acc[m, :] = v
+
+    def stage3(n):
+        acc, zr = getattr(R, "ac" + n), getattr(R, "zr" + n)
+        q = ROWS_OF[n] // 4
+        v = acc[ds(z * q, q), :]
+        for k in (1, 2, 3):
+            recv(zr.at[k - 1], cs[n] + k)
+            v = v + zr[k - 1].astype(F32)
+        gatherA(n, v)
+
+    def piece(n, zz):
+        return regions[n][1](group[n].w[0], group[n].b, zz)
+
+    def gatherA(n, v):
+        p = piece(n, z)
+        p[...] = v.astype(BF)
+        for k in (2, 1, 3):
+            send(p, p, cs[n] + 3 + k, zdev[k])
+
+    def gatherB(n):
+        for k in (1, 2, 3):
+            recv(piece(n, zb[k]), cs[n] + 3 + k)
+        h = regions[n][0](group[n].w[0], group[n].b)
+        send(h, h, cs[n] + 8, group[n].dev[2])
+        send(h, h, cs[n] + 7, group[n].bdev)
+        send(h, h, cs[n] + 9, group[n].dev[1])
+
+    def gatherC(n):
+        h = regions[n][0](group[n].w[0], 1 - group[n].b)
+        recv(h, cs[n] + 7)
+        send(h, h, cs[n] + 10, group[n].dev[2])
+        send(h, h, cs[n] + 11, group[n].dev[1])
+
+    def gatherD(n):
+        h = regions[n][0](group[n].w[2], group[n].b)
+        recv(h, cs[n] + 8)
+        send(h, h, cs[n] + 12, group[n].dev[1])
+
+    def gatherE(n):
+        h = regions[n][0](group[n].w[2], 1 - group[n].b)
+        recv(h, cs[n] + 10)
+        send(h, h, cs[n] + 13, group[n].dev[1])
+
+    def gatherF(n):
+        g = group[n]
+        recv(regions[n][0](g.w[1], g.b), cs[n] + 9)
+        recv(regions[n][0](g.w[1], 1 - g.b), cs[n] + 11)
+        recv(regions[n][0](g.w[3], g.b), cs[n] + 12)
+        recv(regions[n][0](g.w[3], 1 - g.b), cs[n] + 13)
+
+    def heads_in():
+        for k in (1, 2, 3):
+            recv(R.gag.at[zb[k]], cg + k)
+        for h in range(3):
+            R.ga3[h] = jnp.concatenate([R.gag[j, :, 64 * h:64 * h + 64] for j in range(4)], axis=0)
+
+    def backward(h):
+        def part(j, _):
+            qs = ds(j * 256, 256)
+            gah = R.ga3[h, qs, :]
+            p = jnp.concatenate([R.pt[h, 512 * i:512 * i + 512, qs].astype(F32) * R.stat[h, j, i:i + 1, :]
+                                 for i in range(2)], axis=0)
+            pd = p * dot(R.v3[h], gah, 1, 1)
+            gr = (pd - p * colsum(pd)).astype(BF)
+            dk = dot(gr, R.q3[h, qs, :])
+            dv = dot(p.astype(BF), gah)
+            R.dk[...] = R.dk[...] + dk
+            R.dv[...] = R.dv[...] + dv
+            R.half[h, :, qs] = dot(R.k3[h], gr, 0, 0) * 0.125
+            return 0
+
+        R.dk[...] = jnp.zeros((L, HD), F32)
+        R.dv[...] = jnp.zeros((L, HD), F32)
+        lax.fori_loop(0, 2, part, 0)
+        for ref, lo in ((R.dk, 64 * h), (R.dv, 192 + 64 * h)):
+            R.kvs[:, lo:lo + 64] = ref[theirs, :].astype(BF)
+            R.kvo[:, lo:lo + 64] = ref[ours, :]
+
+    ck, cd, cq, ctb, csm, ctz = chan(1), chan(4), cs["q"], cs["t"], chan(6), chan(4)
+    theirs, ours = ds((1 - y) * 512, 512), ds(y * 512, 512)
+
+    def kv_out():
+        send(R.kvs, R.kvr, ck, ydev)
+
+    def kv_in():
+        recv(R.kvr, ck)
+        kv = (R.kvo[...] + R.kvr[...].astype(F32)).astype(BF)
+        gq = jnp.concatenate([R.half[h] for h in range(3)], axis=0).T.astype(BF)
+        R.gqkv[...] = jnp.concatenate([gq, kv], axis=1)
+        for k in (2, 1, 3):
+            send(R.gqkv.at[ds(zk[k] * T, T), :], R.dqin.at[z], cd + k, zdev[k])
+        R.dqin[z] = R.gqkv[ds(z * T, T), :]
+
+    def q0():
+        def other(i, _):
+            R.qs0[ds(i * 128, 128), :] = dot(R.elow[:, ds((1 - c) * 384 + i * 128, 128)], R.gqkv[...], 0, 0).astype(BF)
+            return 0
+
+        def same(i, _):
+            R.qp[ds(i * 128, 128), :] = dot(R.elow[:, ds(c * 384 + i * 128, 128)], R.gqkv[...], 0, 0)
+            return 0
+
+        lax.fori_loop(0, 3, other, 0)
+        send(R.qs0, R.qr0, cq, rdev[1])
+        lax.fori_loop(0, 3, same, 0)
+
+    def q1():
+        recv(R.qr0, cq)
+        R.qs1[...] = (R.qp[ds((1 - x) * 192, 192), :]
+                      + R.qr0[ds((1 - x) * 192, 192), :].astype(F32)).astype(BF)
+        send(R.qs1, R.qr1, cq + 1, rdev[2])
+
+    def qsum(o):
+        return (R.qp[ds(x * 192 + o, 96), :] + R.qr0[ds(x * 192 + o, 96), :].astype(F32)
+                + R.qr1[ds(o, 96), :].astype(F32))
+
+    def q2():
+        recv(R.qr1, cq + 1)
+        R.qs2[...] = qsum((1 - y) * 96).astype(BF)
+        send(R.qs2, R.qr2, cq + 2, ydev)
+
+    def q3():
+        recv(R.qr2, cq + 2)
+        gatherA("q", qsum(y * 96) + R.qr2[...].astype(F32))
+
+    def entry():
+        for k in (1, 2, 3):
+            recv(R.dqin.at[zb[k]], cd + k)
+        gq, gk, gv = (jnp.concatenate([R.dqin[j, :, 192 * i:192 * i + 192] for j in range(4)], axis=1) for i in range(3))
+        R.sm[0:1, :] = colsum(gq.astype(F32))
+        R.sm[1:2, :] = colsum(gv.astype(F32))
+        ge = R.own[...] + dot(gq, R.Gwq[...], 1, 1) + dot(gk, R.Gwk[...], 1, 1) + dot(gv, R.Gwv[...], 1, 1)
+        gel = ge.astype(BF)
+        R.gtok[...] = gel
+        R.gp[...] = dot(hot_of(me, 512, 0), gel)
+        R.sm[12:14, :] = dot(hot_of(me, 16, 512), gel)[0:2, :]
+        R.ts0[...] = R.gp[ds((1 - c) * 256, 256), :].astype(BF)
+        send(R.ts0, R.tr0, ctb, rdev[1])
+        R.sms[0] = R.sm[...]
+        send(R.sms.at[0], R.smr.at[0], csm, rdev[1])
+
+    def t1():
+        recv(R.tr0, ctb)
+        R.ts1[...] = (R.gp[ds(c * 256 + (1 - x) * 128, 128), :]
+                      + R.tr0[ds((1 - x) * 128, 128), :].astype(F32)).astype(BF)
+        send(R.ts1, R.tr1, ctb + 1, rdev[2])
+        recv(R.smr.at[0], csm)
+        R.sms[1] = R.sms[0] + R.smr[0]
+        send(R.sms.at[1], R.smr.at[1], csm + 1, rdev[2])
+
+    def tsum(b):
+        lanes = ds(b * 384, 384)
+        return (R.gp[ds(c * 256 + x * 128, 128), lanes] + R.tr0[ds(x * 128, 128), lanes].astype(F32)
+                + R.tr1[:, lanes].astype(F32))
+
+    def t2():
+        recv(R.tr1, ctb + 1)
+        R.ts2[...] = tsum(1 - y).astype(BF)
+        send(R.ts2, R.tr2, ctb + 2, ydev)
+        recv(R.smr.at[1], csm + 1)
+        R.sms[2] = R.sms[1] + R.smr[1]
+        send(R.sms.at[2], R.smr.at[2], csm + 2, ydev)
+
+    def t3():
+        recv(R.tr2, ctb + 2)
+        tv = tsum(y) + R.tr2[...].astype(F32)
+        R.ts3[...] = tv.astype(BF)
+        for k in (2, 1, 3):
+            send(R.ts3.at[ds(zk[k] * 32, 32), :], R.tr3.at[k], ctz + k, zdev[k])
+        R.gp[0:128, 0:384] = tv
+        recv(R.smr.at[2], csm + 2)
+        R.sms[3] = R.sms[2] + R.smr[2]
+        for k in (2, 1, 3):
+            send(R.sms.at[3], R.smr.at[2 + k], csm + 2 + k, zdev[k])
+
+    def t4():
+        fin = R.gp[ds(z * 32, 32), 0:384]
+        for k in (1, 2, 3):
+            recv(R.tr3.at[k], ctz + k)
+            fin = fin + R.tr3[k].astype(F32)
+        gatherA("t", fin)
+        total = R.sms[3]
+        for k in (1, 2, 3):
+            recv(R.smr.at[2 + k], csm + 2 + k)
+            total = total + R.smr[2 + k]
+        R.Gs[...] = total
+
+    def assemble():
+        gatherF("q")
+
+        def part(i, _):
+            m = ds(i * 128, 128)
+            for t, out in enumerate((R.Gwq, R.Gwk, R.Gwv)):
+                out[m, :] = jnp.concatenate([R.Gq[j, m, 192 * t:192 * t + 192] for j in range(4)], axis=1)
+            return 0
+
+        lax.fori_loop(0, 6, part, 0)
+
+    tasks = {"gs": lambda: pass_on("gs", R.xgs), "gb": lambda: pass_on("gb", R.xgb), "in": heads_in, "kv": kv_out,
+             "vk": kv_in, "q0": q0, "q1": q1, "q2": q2, "q3": q3, "en": entry, "t1": t1, "t2": t2, "t3": t3, "t4": t4,
+             "as": assemble}
+    for h in range(3):
+        tasks["h%d" % h] = partial(backward, h)
+    for n in STREAMS:
+        for stage, f in zip("123ABCDEF", (stage1, stage2, stage3, None, gatherB, gatherC, gatherD, gatherE, gatherF), strict=True):
+            tasks[stage + n] = partial(f, n) if f else None
+    for name in ORDER:
+        tasks[name]()
+    for cp in pending:
+        cp.wait_send()
+
+
+def mega(*args):
+    any_, vm = pl.BlockSpec(memory_space=pltpu.HBM), pl.BlockSpec(memory_space=VMEM)
+    square = VMEM((D, D), BF)
+    return pl.pallas_call(
+        kernel,
+        out_shape=(VMEM((T, D), BF), VMEM((T, D), BF), VMEM((F, D), BF), VMEM((D, F), BF), square, square, square, square,
+                   VMEM((512, D), BF), VMEM((16, D), F32)),
+        in_specs=[any_, any_, vm, vm, any_, vm] + [any_] * 6,
+        out_specs=(vm,) * 10,
+        scratch_shapes=list(scratch().values()),
+        compiler_params=pltpu.CompilerParams(collective_id=0, has_side_effects=True, vmem_limit_bytes=41 << 20),
+    )(*args)
+
+
+def finish_kernel(layer, gtok, g2, g1, go, gq, gk, gv, gt, gs, layer_o, gtok_o, t_o, q_o, k_o, v_o, o_o, o1, o2, tab, buf, wide, sem, sem2):
+    whole = [pltpu.make_async_copy(a, b, sem2.at[i]) for i, (a, b) in enumerate(((layer, layer_o), (gtok, gtok_o)))]
+    for cp in whole:
+        cp.start()
+    tab[0:512, :] = gt[...].astype(F32)
+    tab[512:514, :] = gs[12:14, :]
+    whole.append(pltpu.make_async_copy(tab, t_o, sem2.at[2]))
+    whole[-1].start()
+    chunks = [(g2, o2, buf, i) for i in range(12)] + [(g1, o1, wide, i) for i in range(12)]
+    chunks += [(a, b, buf, i) for a, b in ((go, o_o), (gq, q_o), (gk, k_o), (gv, v_o)) for i in range(3)]
+    flying = {}
+    for n, (src, dst, stage, i) in enumerate(chunks):
+        rows = 256 if stage is buf else 64
+        slot = n % 4
+        if n >= 4:
+            flying[slot].wait()
+        stage[slot] = src[i * rows:(i + 1) * rows, :].astype(F32)
+        flying[slot] = pltpu.make_async_copy(stage.at[slot], dst.at[i * rows:(i + 1) * rows, :], sem.at[slot])
+        flying[slot].start()
+    for slot in range(4):
+        flying[slot].wait()
+    for cp in whole:
+        cp.wait()
+
+
+def finish(*args):
+    S = jax.ShapeDtypeStruct
+    square = S((D, D), F32)
+    hbm, vm = pl.BlockSpec(memory_space=pltpu.HBM), pl.BlockSpec(memory_space=VMEM)
+    return pl.pallas_call(
+        finish_kernel,
+        out_shape=(S((T, D), BF), S((T, D), BF), S((514, D), F32), square, square, square, square, S((D, F), F32), S((F, D), F32)),
+        in_specs=[vm] * 10,
+        out_specs=(hbm,) * 9,
+        scratch_shapes=[VMEM((514, D), F32), VMEM((4, 256, D), F32), VMEM((4, 64, F), F32), pltpu.SemaphoreType.DMA((4,)),
+                        pltpu.SemaphoreType.DMA((3,))],
+        compiler_params=pltpu.CompilerParams(vmem_limit_bytes=20 << 20),
+    )(*args)
+
+
+def fast_device(tokens, cotangent, segment_ids, restarts, position_table, query_weight, query_bias, key_weight,
+                value_weight, value_bias, out_weight, out_bias, first_gain, first_shift, inner_weight, inner_bias,
+                outer_weight, outer_bias, second_gain, second_shift):
+    vectors = (query_bias, value_bias, out_bias, first_gain, first_shift, outer_bias, second_gain, second_shift)
+    small, at = jnp.zeros((16 * D,), F32), 0
+    for v in vectors + (inner_bias,):
+        small = small + jnp.pad(v.astype(F32), (at, 16 * D - at - v.shape[0]))
+        at += v.shape[0]
+    small = small.reshape(16, D)
+    made = mega(
+        tokens[0], cotangent[0], segment_ids, restarts, position_table, small, query_weight,
+        key_weight, value_weight, out_weight, inner_weight, outer_weight)
+    layer, gtok, table, gq, gk, gv, go, g1, g2 = finish(*made)
+    gs = made[-1]
+    return (layer[None], gtok[None], table, gq, gs[0], gk, gv, gs[1], go, gs[2], gs[3], gs[4], g1, gs[8:12].reshape(F), g2,
+            gs[5], gs[6], gs[7])
+
 
 HEADS = 12
 
@@ -433,6 +1166,7 @@
         P(),
         P(),
     )
+    body = fast_device if mesh.shape["seq"] == 8 and mesh.shape["rows"] == 4 else per_device
     return jax.shard_map(
-        per_device, mesh=mesh, in_specs=in_specs, out_specs=out_specs, check_vma=False
-    )
+        body, mesh=mesh, in_specs=in_specs, out_specs=out_specs, check_vma=False
+    )

time: 1460 us -> 217 us (0.15)
  waiting for transfers between devices: 1230 us -> 0 us
  Pallas kernels: 0 us -> 212 us
  blocking collectives: 72 us -> 0 us
  matrix products: 67.5 us -> 0 us
  other arithmetic: 43.3 us -> 0.83 us
  local copies, waits for them, and re-layouts: 22.7 us -> 1.91 us
    reduce_scatter x8 -> x0, waiting for transfers between devices: 728 us -> none  [the longest x1 165 us: per_device(): lax.psum_scatter(grad_winner, 'seq', scatter_dimension=0, tiled=True)]
    all_gather x8 -> x0, waiting for transfers between devices: 323 us -> none  [the longest x1 78.1 us: per_device(): lax.all_gather(pieces[4].astype(jnp.bfloat16), 'seq', axis=0, tiled=True)]
    pallas_call x0 -> x2, Pallas kernels: none -> 212 us  [the longest x1 202 us: mega(): pl.pallas_call(kernel, out_shape=(VMEM((T, D), BF), VMEM((T, D), BF), VME...]
    psum x2 -> x0, waiting for transfers between devices: 177 us -> none  [the longest x1 129 us: per_device(): lax.psum((grad_table, grad_bquery, grad_bvalue, grad_bout, grad_gfirst, g...]
    dot_general x26 -> x0, matrix products: 67.5 us -> none  [the longest x6 20 us: outer_sum(): lax.dot_general(left, right, (((0,), (0,)), ((), ())), preferred_element_...]
    psum x1 -> x0, blocking collectives: 41.3 us -> none  [per_device(): lax.psum((grad_table, grad_bquery, grad_bvalue, grad_bout, grad_gfirst, g...]
    convert_element_type x21 -> x0, other arithmetic: 36.5 us -> none  [the longest x1 7.37 us: per_device(): lax.all_gather(pieces[4].astype(jnp.bfloat16), 'seq', axis=0, tiled=True)]
    all_gather x1 -> x0, blocking collectives: 17.7 us -> none  [per_device(): lax.all_gather(segment_ids, 'seq', axis=1, tiled=True)]
  transfers between devices with their start and end apart: 18 -> 0, of which waited for: 17 -> 0; matrix products, arithmetic and copies ran while one was open for 5% -> 0% of each run, Pallas kernels for 0% -> 0%
where the time goes in v2:
time: 217 us; the launch traced here: 215 us
  Pallas kernels  212 us (98%)
    pallas_call x1, Pallas kernels, mega(): pl.pallas_call(kernel, out_shape=(VMEM((T, D), BF), VMEM((T, D), BF), VME...  202 us
    pallas_call x1, Pallas kernels, finish(): pl.pallas_call(finish_kernel, out_shape=(S((T, D), BF), S((T, D), BF), S(...  9.95 us

profile of v2, /device:TPU:0, one launch (start us, length us, event | category | flops | bytes accessed | tf_op | source)
XLA Modules:
  0.0 215.2 jit_solution(8281507764051653812)
XLA Ops:
  0.7 0.8 convert_add_fusion
  1.5 0.6 reshape.42.refs_5_
  2.1 201.9 %shard_map.331 = (bf16[128,768]{1,0:T(8,128)(2,1)S(1)}, bf16[128,768]{1,0:T(8,128)(2,1)S(1)}, bf16[3072,768]{1,0:T(8,128)(2,1)S(1)}, bf16[768,3072]{1,0:T(8,128)...) custom-call(bf16[128,768]{1,0:T(8,128)(2,1)} %bitcast.4, ...), custom_call_target="tpu_custom_call" | custom-call | tf_op jit(solution)/shard_map/pallas_call | solution.py:672
  204.0 9.9 %shard_map.332 = (bf16[128,768]{1,0:T(8,128)(2,1)}, bf16[128,768]{1,0:T(8,128)(2,1)}, f32[514,768]{1,0:T(8,128)}, f32[768,768]{1,0:T(8,128)}, f32[768,768]{1,0:T...) custom-call(bf16[128,768]{1,0:T(8,128)(2,1)S(1)} %get-tuple-element.37.layer, ...), custom_call_target="tpu_custom_call" | custom-call | tf_op jit(solution)/shard_map/pallas_call | solution.py:712
  214.0 0.7 slice_reduce_fusion
  214.6 0.6 reshape.43
  (1 shorter events, 0.0 us)

commit v3 on v2

--- a/solution.py
+++ b/solution.py
@@ -17,10 +17,12 @@
 ROWS_OF = {"2a": 384, "2b": 384, "1a": 384, "1b": 384, "o": 192}
 STREAMS = tuple(ROWS_OF) + ("q", "t")
 ORDER = (
-    "gs", "12a", "12b", "in", "h0", "11a", "11b", "gb", "h1", "22a", "1o", "h2", "kv", "21a", "22b", "21b", "32a", "vk", "q0",
-    "2o", "31a", "q1", "32b", "B2a", "31b", "3o", "B1a", "q2", "en", "C2a", "C1a", "D2a", "D1a", "B2b", "B1b", "t1", "q3",
-    "Bo", "C2b", "C1b", "E2a", "E1a", "t2", "Co", "Bq", "t3", "D2b", "D1b", "Do", "t4", "Cq", "E2b", "E1b", "Eo", "Bt", "Dq",
-    "Ct", "Eq", "Dt", "Et", "F2a", "F1a", "F2b", "F1b", "Fo", "as", "Ft")
+    "sb", "gs", "in", "11b", "12b", "11a", "h0", "h1", "12a", "21b", "gb", "h2", "22b", "z1b", "21a", "1o", "31b",
+    "z2b", "kv", "z1a", "A1b", "32b", "2o", "B1b", "A2b", "vk", "q0", "q1", "B2b", "31a", "C2b", "D1b", "q2", "C1b",
+    "en", "A1a", "zo", "q3", "t1", "B1a", "E1b", "Aq", "t2", "3o", "22a", "Bq", "Ao", "t3", "E2b", "Bo", "z2a", "Cq",
+    "t4", "32a", "F1b", "C1a", "At", "A2a", "Do", "B2a", "D2b", "Eq", "Co", "Bt", "E1a", "C2a", "Dq", "Eo", "Ct",
+    "Fo", "as", "Dt", "Et", "D2a", "D1a", "F2b", "E2a", "F1a", "Ft", "F2a",
+)
 
 
 def dot(a, b, ca=1, cb=0):
@@ -100,8 +102,7 @@
     R = SimpleNamespace(**dict(zip(names, refs, strict=True)))
     seq, row = lax.axis_index("seq"), lax.axis_index("rows")
     z, y, x, c = seq // 2, seq % 2, row // 2, row % 2
-    zk = [(z + k) % 4 for k in range(4)]
-    zb = [(z + 4 - k) % 4 for k in range(4)]
+    zk = [z, z + 1 - 2 * (z % 2), (z + 2) % 4, 3 - z]
     rk = [row, x * 2 + (1 - c), (1 - x) * 2 + c, (1 - x) * 2 + (1 - c)]
     zdev = [(zk[k] * 2 + y, row) for k in range(4)]
     ydev = (z * 2 + (1 - y), row)
@@ -130,29 +131,30 @@
     wy = y * 2 + c
     gy = SimpleNamespace(w=[wy, y * 2 + (1 - c), (1 - y) * 2 + c, (1 - y) * 2 + (1 - c)],
                          dev=[(seq, row), rdev[1], ydev, yxdev], b=x, bdev=rdev[2])
-    group = {n: gy if n[0] in "1o" else gx for n in STREAMS}
+    group = {n: gy if n[0] in "1ot" else gx for n in STREAMS}
     group.update(first=gy, gi=gy, att=gy, gb=gy, act=gx, gs=gx)
 
-    loads = {}
-    weights = (("n", R.tokens, R.tok.at[y * 4 + z]), ("t", R.htable, R.table), ("k", R.hk, R.Gwk), ("v", R.hv, R.Gwv), ("q", R.hq, R.Gwq), ("c", R.hcot, R.cot), ("o", R.ho, R.Go), ("1", R.h1, R.G1), ("2", R.h2, R.G2))
-
-    def load(i):
-        n, src, dst = weights[i]
-        loads[n] = pltpu.make_async_copy(src, dst, R.wsem.at[i])
-        loads[n].start()
-
-    for i in range(5):
-        load(i)
-
-    me = y * 4 + z
-    R.meta[me] = jnp.zeros((8, T), I32)
-    R.meta[me, 0:1, :] = R.rests[...]
-    R.meta[me, 1:2, :] = R.segs[...]
     seqpeers = [zdev[1], zdev[2], zdev[3]] + [(zk[k] * 2 + (1 - y), row) for k in range(4)]
     peers = seqpeers + rdev[1:] + [yxdev]
     bar = pltpu.get_barrier_semaphore()
     for p in peers:
         pl.semaphore_signal(bar, inc=1, device_id=p, device_id_type=MESH)
+
+    loads = {}
+    weights = (("n", R.tokens, R.tok.at[y * 4 + z]), ("t", R.htable, R.table), ("k", R.hk, R.Gwk), ("v", R.hv, R.Gwv), ("q", R.hq, R.Gwq), ("c", R.hcot, R.cot), ("o", R.ho, R.Go), ("1", R.h1, R.G1), ("2", R.h2, R.G2))
+
+    def load(i):
+        n, src, dst = weights[i]
+        loads[n] = pltpu.make_async_copy(src, dst, R.wsem.at[i])
+        loads[n].start()
+
+    for i in range(5):
+        load(i)
+
+    me = y * 4 + z
+    R.meta[me] = jnp.zeros((8, T), I32)
+    R.meta[me, 0:1, :] = R.rests[...]
+    R.meta[me, 1:2, :] = R.segs[...]
     pl.semaphore_wait(bar, len(peers))
     loads["n"].wait()
     cm = chan(7)
@@ -168,8 +170,8 @@
         tokens_out.append(copy(R.tok.at[b], R.tok.at[b], i, dev))
         tokens_out[-1].start()
 
-    for k in (1, 2, 3):
-        forward(me, ct + k, zdev[k])
+    forward(me, ct + 1, zdev[1])
+    forward(me, ct + 2, zdev[2])
     forward(me, ct + 4, ydev)
     for i in range(5, 9):
         load(i)
@@ -233,8 +235,10 @@
     R.own[...] = block(me, True)
 
     for k in (1, 2, 3):
-        b = y * 4 + zb[k]
+        b = y * 4 + zk[k]
         recv(R.tok.at[b], ct + k)
+        if k == 2:
+            forward(b, ct + 3, zdev[1])
         forward(b, ct + 4 + k, ydev)
         block(b, True)
 
@@ -273,7 +277,7 @@
 
     lax.fori_loop(0, 6, attend_near, 0)
     for k in (0, 1, 2, 3):
-        b = (1 - y) * 4 + zb[k]
+        b = (1 - y) * 4 + zk[k]
         recv(R.tok.at[b], ct + 4 + k)
         block(b, False)
     lax.fori_loop(0, 6, attend_far, 0)
@@ -288,7 +292,7 @@
     for cp in tokens_out:
         cp.wait_send()
     for k in (1, 2, 3):
-        recv(R.attg.at[zb[k]], ca + k)
+        recv(R.attg.at[zk[k]], ca + k)
 
     def slot(n, k):
         return ds(group[n].w[k] * T, T)
@@ -337,8 +341,6 @@
         else:
             R.xact[slot("act", 0), :] = act
         second = second + dot(act, R.G2[cols, :])
-    for k in (1, 2, 3):
-        send(R.attg.at[gy.w[k]], R.xatt.at[:, slot("att", 0)], cx["att"] + k, gy.dev[k])
     R.xatt[:, slot("att", 0)] = R.attg[gy.w[0]]
     u = first + second + small(5)
     u = u - mean(u)
@@ -380,7 +382,6 @@
     for k in (2, 1, 3):
         send(R.gaout.at[zk[k]], R.gag.at[z], cg + k, zdev[k])
     R.gag[z] = R.gaout[z]
-    share("gb", R.xgb)
     R.sm[2:3, :] = colsum(gb.astype(F32))
 
     def two(h):
@@ -446,22 +447,30 @@
         acc, br, zr = (getattr(R, a + n) for a in ("ac", "br", "zr"))
         recv(br, cs[n])
         q = ROWS_OF[n] // 4
-        for k in (2, 1, 3, 0):
+        for k in (3, 1, 2, 0):
             m = ds(zk[k] * q, q)
             v = acc[m, :] + br[m, :].astype(F32)
-            if k:
+            if k % 2:
                 br[m, :] = v.astype(BF)
-                send(br.at[m, :], zr.at[k - 1], cs[n] + k, zdev[k])
+                send(br.at[m, :], zr.at[k // 2], cs[n] + 1 + k // 2, zdev[1])
             else:
                 acc[m, :] = v
+
+    def stage2z(n):
+        acc, br, zr = (getattr(R, a + n) for a in ("ac", "br", "zr"))
+        recv(zr.at[1], cs[n] + 2)
+        q = ROWS_OF[n] // 4
+        m = ds(zk[2] * q, q)
+        br[m, :] = (acc[m, :] + zr[1].astype(F32)).astype(BF)
+        send(br.at[m, :], zr.at[2], cs[n] + 3, zdev[2])
 
     def stage3(n):
         acc, zr = getattr(R, "ac" + n), getattr(R, "zr" + n)
         q = ROWS_OF[n] // 4
         v = acc[ds(z * q, q), :]
-        for k in (1, 2, 3):
-            recv(zr.at[k - 1], cs[n] + k)
-            v = v + zr[k - 1].astype(F32)
+        for i in (0, 2):
+            recv(zr.at[i], cs[n] + 1 + i)
+            v = v + zr[i].astype(F32)
         gatherA(n, v)
 
     def piece(n, zz):
@@ -470,12 +479,17 @@
     def gatherA(n, v):
         p = piece(n, z)
         p[...] = v.astype(BF)
-        for k in (2, 1, 3):
-            send(p, p, cs[n] + 3 + k, zdev[k])
+        send(p, p, cs[n] + 5, zdev[2])
+        send(p, p, cs[n] + 4, zdev[1])
+
+    def gatherZ(n):
+        p = piece(n, zk[2])
+        recv(p, cs[n] + 5)
+        send(p, p, cs[n] + 6, zdev[1])
 
     def gatherB(n):
-        for k in (1, 2, 3):
-            recv(piece(n, zb[k]), cs[n] + 3 + k)
+        for k in (1, 3):
+            recv(piece(n, zk[k]), cs[n] + 3 + k)
         h = regions[n][0](group[n].w[0], group[n].b)
         send(h, h, cs[n] + 8, group[n].dev[2])
         send(h, h, cs[n] + 7, group[n].bdev)
@@ -504,9 +518,14 @@
         recv(regions[n][0](g.w[3], g.b), cs[n] + 12)
         recv(regions[n][0](g.w[3], 1 - g.b), cs[n] + 13)
 
+    def share_branch():
+        for k in (1, 2, 3):
+            send(R.attg.at[gy.w[k]], R.xatt.at[:, slot("att", 0)], cx["att"] + k, gy.dev[k])
+        share("gb", R.xgb)
+
     def heads_in():
         for k in (1, 2, 3):
-            recv(R.gag.at[zb[k]], cg + k)
+            recv(R.gag.at[zk[k]], cg + k)
         for h in range(3):
             R.ga3[h] = jnp.concatenate([R.gag[j, :, 64 * h:64 * h + 64] for j in range(4)], axis=0)
 
@@ -581,7 +600,7 @@
 
     def entry():
         for k in (1, 2, 3):
-            recv(R.dqin.at[zb[k]], cd + k)
+            recv(R.dqin.at[zk[k]], cd + k)
         gq, gk, gv = (jnp.concatenate([R.dqin[j, :, 192 * i:192 * i + 192] for j in range(4)], axis=1) for i in range(3))
         R.sm[0:1, :] = colsum(gq.astype(F32))
         R.sm[1:2, :] = colsum(gv.astype(F32))
@@ -595,31 +614,34 @@
         R.sms[0] = R.sm[...]
         send(R.sms.at[0], R.smr.at[0], csm, rdev[1])
 
+    gt = group["t"]
+
     def t1():
         recv(R.tr0, ctb)
-        R.ts1[...] = (R.gp[ds(c * 256 + (1 - x) * 128, 128), :]
-                      + R.tr0[ds((1 - x) * 128, 128), :].astype(F32)).astype(BF)
-        send(R.ts1, R.tr1, ctb + 1, rdev[2])
+        a = gt.w[0] // 2
+        R.ts1[...] = (R.gp[ds(c * 256 + (1 - a) * 128, 128), :]
+                      + R.tr0[ds((1 - a) * 128, 128), :].astype(F32)).astype(BF)
+        send(R.ts1, R.tr1, ctb + 1, gt.dev[2])
         recv(R.smr.at[0], csm)
         R.sms[1] = R.sms[0] + R.smr[0]
         send(R.sms.at[1], R.smr.at[1], csm + 1, rdev[2])
 
     def tsum(b):
-        lanes = ds(b * 384, 384)
-        return (R.gp[ds(c * 256 + x * 128, 128), lanes] + R.tr0[ds(x * 128, 128), lanes].astype(F32)
+        lanes, a = ds(b * 384, 384), gt.w[0] // 2
+        return (R.gp[ds(c * 256 + a * 128, 128), lanes] + R.tr0[ds(a * 128, 128), lanes].astype(F32)
                 + R.tr1[:, lanes].astype(F32))
 
     def t2():
         recv(R.tr1, ctb + 1)
-        R.ts2[...] = tsum(1 - y).astype(BF)
-        send(R.ts2, R.tr2, ctb + 2, ydev)
+        R.ts2[...] = tsum(1 - gt.b).astype(BF)
+        send(R.ts2, R.tr2, ctb + 2, gt.bdev)
         recv(R.smr.at[1], csm + 1)
         R.sms[2] = R.sms[1] + R.smr[1]
         send(R.sms.at[2], R.smr.at[2], csm + 2, ydev)
 
     def t3():
         recv(R.tr2, ctb + 2)
-        tv = tsum(y) + R.tr2[...].astype(F32)
+        tv = tsum(gt.b) + R.tr2[...].astype(F32)
         R.ts3[...] = tv.astype(BF)
         for k in (2, 1, 3):
             send(R.ts3.at[ds(zk[k] * 32, 32), :], R.tr3.at[k], ctz + k, zdev[k])
@@ -652,14 +674,14 @@
 
         lax.fori_loop(0, 6, part, 0)
 
-    tasks = {"gs": lambda: pass_on("gs", R.xgs), "gb": lambda: pass_on("gb", R.xgb), "in": heads_in, "kv": kv_out,
+    tasks = {"gs": lambda: pass_on("gs", R.xgs), "gb": lambda: pass_on("gb", R.xgb), "sb": share_branch, "in": heads_in, "kv": kv_out,
              "vk": kv_in, "q0": q0, "q1": q1, "q2": q2, "q3": q3, "en": entry, "t1": t1, "t2": t2, "t3": t3, "t4": t4,
              "as": assemble}
     for h in range(3):
         tasks["h%d" % h] = partial(backward, h)
     for n in STREAMS:
-        for stage, f in zip("123ABCDEF", (stage1, stage2, stage3, None, gatherB, gatherC, gatherD, gatherE, gatherF), strict=True):
-            tasks[stage + n] = partial(f, n) if f else None
+        for stage, f in zip("12z3ABCDEF", (stage1, stage2, stage2z, stage3, gatherZ, gatherB, gatherC, gatherD, gatherE, gatherF), strict=True):
+            tasks[stage + n] = partial(f, n)
     for name in ORDER:
         tasks[name]()
     for cp in pending:

time: 217 us -> 184 us (0.85)
  Pallas kernels: 212 us -> 179 us
    pallas_call x1, Pallas kernels: 202 us -> 169 us  [mega(): pl.pallas_call(kernel, out_shape=(VMEM((T, D), BF), VMEM((T, D), BF), VME...]
where the time goes in v3:
time: 184 us; the launch traced here: 182 us
  Pallas kernels  179 us (97%)
  local copies, waits for them, and re-layouts  1.91 us (1%)
    pallas_call x1, Pallas kernels, mega(): pl.pallas_call(kernel, out_shape=(VMEM((T, D), BF), VMEM((T, D), BF), VME...  169 us
    pallas_call x1, Pallas kernels, finish(): pl.pallas_call(finish_kernel, out_shape=(S((T, D), BF), S((T, D), BF), S(...  9.95 us

profile of v3, /device:TPU:0, one launch (start us, length us, event | category | flops | bytes accessed | tf_op | source)
XLA Modules:
  0.0 182.3 jit_solution(13490716781535017682)
XLA Ops:
  0.7 0.8 convert_add_fusion
  1.5 0.6 reshape.42.refs_5_
  2.1 168.9 %shard_map.331 = (bf16[128,768]{1,0:T(8,128)(2,1)S(1)}, bf16[128,768]{1,0:T(8,128)(2,1)S(1)}, bf16[3072,768]{1,0:T(8,128)(2,1)S(1)}, bf16[768,3072]{1,0:T(8,128)...) custom-call(bf16[128,768]{1,0:T(8,128)(2,1)} %bitcast.4, ...), custom_call_target="tpu_custom_call" | custom-call | tf_op jit(solution)/shard_map/pallas_call | solution.py:694
  171.1 9.9 %shard_map.332 = (bf16[128,768]{1,0:T(8,128)(2,1)}, bf16[128,768]{1,0:T(8,128)(2,1)}, f32[514,768]{1,0:T(8,128)}, f32[768,768]{1,0:T(8,128)}, f32[768,768]{1,0:T...) custom-call(bf16[128,768]{1,0:T(8,128)(2,1)S(1)} %get-tuple-element.37.layer, ...), custom_call_target="tpu_custom_call" | custom-call | tf_op jit(solution)/shard_map/pallas_call | solution.py:734
  181.0 0.7 slice_reduce_fusion
  181.7 0.6 reshape.43
  (1 shorter events, 0.0 us)

commit v4 on v3

--- a/solution.py
+++ b/solution.py
@@ -13,7 +13,7 @@
 BF, F32, I32 = jnp.bfloat16, jnp.float32, jnp.int32
 T, D, F, L, HD = 128, 768, 3072, 1024, 64
 EPS = 1e-5
-CHANNELS = 220
+CHANNELS = 240
 ROWS_OF = {"2a": 384, "2b": 384, "1a": 384, "1b": 384, "o": 192}
 STREAMS = tuple(ROWS_OF) + ("q", "t")
 ORDER = (
@@ -163,16 +163,21 @@
         cp = copy(R.meta.at[me], R.meta.at[me], cm + i, dev)
         cp.start()
         metas.append(cp)
-    ct = chan(8)
+    ct = chan(16)
     tokens_out = []
 
-    def forward(b, i, dev):
-        tokens_out.append(copy(R.tok.at[b], R.tok.at[b], i, dev))
+    def half_of(b, h):
+        return R.tok.at[b, 64 * h:64 * h + 64, :]
+
+    def forward(b, i, h, dev):
+        tokens_out.append(copy(half_of(b, h), half_of(b, h), ct + 2 * i + h, dev))
         tokens_out[-1].start()
 
-    forward(me, ct + 1, zdev[1])
-    forward(me, ct + 2, zdev[2])
-    forward(me, ct + 4, ydev)
+    for h in range(2):
+        forward(me, 1, h, zdev[1])
+        forward(me, 4, h, ydev)
+    for h in range(2):
+        forward(me, 2, h, zdev[2])
     for i in range(5, 9):
         load(i)
     loads["t"].wait()
@@ -236,10 +241,11 @@
 
     for k in (1, 2, 3):
         b = y * 4 + zk[k]
-        recv(R.tok.at[b], ct + k)
-        if k == 2:
-            forward(b, ct + 3, zdev[1])
-        forward(b, ct + 4 + k, ydev)
+        for h in range(2):
+            recv(half_of(b, h), ct + 2 * k + h)
+            if k == 2:
+                forward(b, 3, h, zdev[1])
+            forward(b, 4 + k, h, ydev)
         block(b, True)
 
     def scores(h, j, parity):
@@ -278,21 +284,28 @@
     lax.fori_loop(0, 6, attend_near, 0)
     for k in (0, 1, 2, 3):
         b = (1 - y) * 4 + zk[k]
-        recv(R.tok.at[b], ct + 4 + k)
+        for h in range(2):
+            recv(half_of(b, h), ct + 8 + 2 * k + h)
         block(b, False)
-    lax.fori_loop(0, 6, attend_far, 0)
-    for j in range(4):
-        R.attcat[j] = jnp.concatenate([R.half[h, :, j * T:(j + 1) * T] for h in range(3)], axis=0).astype(BF)
-    ca = chan(4)
-    for k in (2, 1, 3):
-        send(R.attcat.at[zk[k]], R.attg.at[z], ca + k, zdev[k])
+    ca = chan(12)
+
+    def head_of(ref, j, h):
+        return ref.at[j, 64 * h:64 * h + 64, :]
+
+    for h in range(3):
+        lax.fori_loop(2 * h, 2 * h + 2, attend_far, 0)
+        for j in range(4):
+            R.attcat[j, 64 * h:64 * h + 64, :] = R.half[h, :, j * T:(j + 1) * T].astype(BF)
+        for k in (2, 1, 3):
+            send(head_of(R.attcat, zk[k], h), head_of(R.attg, z, h), ca + 3 * k + h, zdev[k])
     R.attg[z] = R.attcat[z]
     for n in "co12":
         loads[n].wait()
     for cp in tokens_out:
         cp.wait_send()
     for k in (1, 2, 3):
-        recv(R.attg.at[zk[k]], ca + k)
+        for h in range(3):
+            recv(head_of(R.attg, zk[k], h), ca + 3 * k + h)
 
     def slot(n, k):
         return ds(group[n].w[k] * T, T)

time: 184 us -> 182 us (0.989)
  no operation moved by 1% of the time
where the time goes in v4:
time: 182 us; the launch traced here: 181 us
  Pallas kernels  178 us (98%)
  local copies, waits for them, and re-layouts  1.91 us (1%)
    pallas_call x1, Pallas kernels, mega(): pl.pallas_call(kernel, out_shape=(VMEM((T, D), BF), VMEM((T, D), BF), VME...  168 us
    pallas_call x1, Pallas kernels, finish(): pl.pallas_call(finish_kernel, out_shape=(S((T, D), BF), S((T, D), BF), S(...  9.95 us

profile of v4, /device:TPU:0, one launch (start us, length us, event | category | flops | bytes accessed | tf_op | source)
XLA Modules:
  0.0 181.4 jit_solution(17126161298275840630)
XLA Ops:
  0.7 0.8 convert_add_fusion
  1.5 0.6 reshape.42.refs_5_
  2.1 168.0 %shard_map.331 = (bf16[128,768]{1,0:T(8,128)(2,1)S(1)}, bf16[128,768]{1,0:T(8,128)(2,1)S(1)}, bf16[3072,768]{1,0:T(8,128)(2,1)S(1)}, bf16[768,3072]{1,0:T(8,128)...) custom-call(bf16[128,768]{1,0:T(8,128)(2,1)} %bitcast.4, ...), custom_call_target="tpu_custom_call" | custom-call | tf_op jit(solution)/shard_map/pallas_call | solution.py:707
  170.2 9.9 %shard_map.332 = (bf16[128,768]{1,0:T(8,128)(2,1)}, bf16[128,768]{1,0:T(8,128)(2,1)}, f32[514,768]{1,0:T(8,128)}, f32[768,768]{1,0:T(8,128)}, f32[768,768]{1,0:T...) custom-call(bf16[128,768]{1,0:T(8,128)(2,1)S(1)} %get-tuple-element.37.layer, ...), custom_call_target="tpu_custom_call" | custom-call | tf_op jit(solution)/shard_map/pallas_call | solution.py:747
  180.1 0.7 slice_reduce_fusion
  180.8 0.6 reshape.43
  (1 shorter events, 0.0 us)

commit v5 on v4

--- a/solution.py
+++ b/solution.py
@@ -17,11 +17,11 @@
 ROWS_OF = {"2a": 384, "2b": 384, "1a": 384, "1b": 384, "o": 192}
 STREAMS = tuple(ROWS_OF) + ("q", "t")
 ORDER = (
-    "sb", "gs", "in", "11b", "12b", "11a", "h0", "h1", "12a", "21b", "gb", "h2", "22b", "z1b", "21a", "1o", "31b",
-    "z2b", "kv", "z1a", "A1b", "32b", "2o", "B1b", "A2b", "vk", "q0", "q1", "B2b", "31a", "C2b", "D1b", "q2", "C1b",
-    "en", "A1a", "zo", "q3", "t1", "B1a", "E1b", "Aq", "t2", "3o", "22a", "Bq", "Ao", "t3", "E2b", "Bo", "z2a", "Cq",
-    "t4", "32a", "F1b", "C1a", "At", "A2a", "Do", "B2a", "D2b", "Eq", "Co", "Bt", "E1a", "C2a", "Dq", "Eo", "Ct",
-    "Fo", "as", "Dt", "Et", "D2a", "D1a", "F2b", "E2a", "F1a", "Ft", "F2a",
+    "sb", "gs", "11a", "in", "12a", "h0", "h1", "gb", "11b", "21a", "22a", "h2", "z1a", "21b", "kv", "12b", "1o",
+    "z2a", "31a", "A1a", "32a", "B1a", "z1b", "A2a", "vk", "q0", "q1", "B2a", "31b", "C2a", "2o", "q2", "C1a", "en",
+    "A1b", "q3", "t1", "B1b", "Aq", "E2a", "22b", "zo", "t2", "Bq", "3o", "z2b", "Ao", "32b", "D2a", "D1b", "C1b",
+    "t3", "Bo", "Cq", "A2b", "Co", "B2b", "t4", "E1b", "Dq", "Eo", "At", "F2a", "Do", "Eq", "Bt", "C2b", "D1a", "Dt",
+    "Ct", "as", "D2b", "E1a", "F1b", "Et", "Fo", "Ft", "E2b", "F1a", "F2b",
 )
 
 

time: 182 us -> 178 us (0.978)
  Pallas kernels: 178 us -> 174 us
    pallas_call x1, Pallas kernels: 168 us -> 164 us  [mega(): pl.pallas_call(kernel, out_shape=(VMEM((T, D), BF), VMEM((T, D), BF), VME...]
where the time goes in v5:
time: 178 us
  Pallas kernels  174 us (98%)
  local copies, waits for them, and re-layouts  1.91 us (1%)
    pallas_call x1, Pallas kernels, mega(): pl.pallas_call(kernel, out_shape=(VMEM((T, D), BF), VMEM((T, D), BF), VME...  164 us
    pallas_call x1, Pallas kernels, finish(): pl.pallas_call(finish_kernel, out_shape=(S((T, D), BF), S((T, D), BF), S(...  9.95 us

profile of v5, /device:TPU:0, one launch (start us, length us, event | category | flops | bytes accessed | tf_op | source)
XLA Modules:
  0.0 177.7 jit_solution(5812701530272606535)
XLA Ops:
  0.7 0.8 convert_add_fusion
  1.5 0.6 reshape.42.refs_5_
  2.1 164.3 %shard_map.331 = (bf16[128,768]{1,0:T(8,128)(2,1)S(1)}, bf16[128,768]{1,0:T(8,128)(2,1)S(1)}, bf16[3072,768]{1,0:T(8,128)(2,1)S(1)}, bf16[768,3072]{1,0:T(8,128)...) custom-call(bf16[128,768]{1,0:T(8,128)(2,1)} %bitcast.4, ...), custom_call_target="tpu_custom_call" | custom-call | tf_op jit(solution)/shard_map/pallas_call | solution.py:707
  166.4 9.9 %shard_map.332 = (bf16[128,768]{1,0:T(8,128)(2,1)}, bf16[128,768]{1,0:T(8,128)(2,1)}, f32[514,768]{1,0:T(8,128)}, f32[768,768]{1,0:T(8,128)}, f32[768,768]{1,0:T...) custom-call(bf16[128,768]{1,0:T(8,128)(2,1)S(1)} %get-tuple-element.37.layer, ...), custom_call_target="tpu_custom_call" | custom-call | tf_op jit(solution)/shard_map/pallas_call | solution.py:747
  176.4 0.7 slice_reduce_fusion
  177.0 0.6 reshape.43
  (1 shorter events, 0.0 us)
